TPU v7x, 256 devices: a whole 4x4x8 slice. The times are simulated.
256 devices in a mesh: tm: 32 (over x_hi, z, core), space: 8 (over y, x_lo).
Axes of the slice: x: 4 (x_hi: 2, x_lo: 2; x = x_hi * 2 + x_lo), y: 4, z: 8, core: 2. Of those that a mesh axis runs over, the one named last changes fastest.
Arguments:
- queries: bfloat16 [32768, 1536], P(('tm', 'space')), may hold values from -24 to 24
- keys: bfloat16 [32768, 1536], P(('tm', 'space')), may hold values from -24 to 24
- values: bfloat16 [32768, 1536], P(('tm', 'space')), may hold values from -8 to 8
- tile_mask: int32 [32, 32], replicated, may hold values from 0 to 1, as said below
- inner_x: bfloat16 [32768, 1536], P(('tm', 'space')), may hold values from -140 to 140
- bc_proj: bfloat16 [32768, 128], P(('tm', 'space')), may hold values from -4 to 4
- log_decay: bfloat16 [24, 32768], P(None, ('tm', 'space')), may hold values from -1 to 0
- col_order: int32 [32], replicated, may hold values from 0 to 31, each once
- norm_gain: float32 [1536], replicated, may hold values from 0.1 to 1.9
Outputs:
- mixed: bfloat16 [32768, 1536], P(('tm', 'space'))
Inputs may be any that keep to these rules, and one draw needn't show every extreme that they name: `tile_mask`: 1 on the diagonal and for frames exactly 8 before or after around the loop; 0 for frames more than 8 away around the loop.
All inputs are finite; a program needn't handle non-finite values.
Results may differ from a plain program's by a relative error of at most 0.017.
Values may be sent and summed in bfloat16 or wider, within the bound.
No kernel may reach another device: no remote copies, remote signals or barrier semaphores. Data moves between devices by JAX's collectives and lax.ppermute only.
A program may use at most 384 MiB of HBM per device.

v0:
```python
import functools
import math

import jax
import jax.numpy as jnp
from jax import lax
from jax.experimental import pallas as pl
from jax.experimental.pallas import tpu as pltpu
from jax.sharding import PartitionSpec as P

HEADS = 12
HEAD_DIM = 128
SCAN_HEADS = 24
SCAN_DIM = 64
STATE_DIM = 64
COLS = 32
TOKENS = 128
N_TM = 32
N_SPACE = 8
GROUP = HEADS // 4 * HEAD_DIM
WIN = 256
ROWS = STATE_DIM + 8

COST = 0.1
EPS = 1e-05
FLOOR = -1e30
LOG2_SCALE = HEAD_DIM ** (-0.5) * math.log2(math.e)
BF16 = jnp.bfloat16
F32 = jnp.float32

VMEM = pl.BlockSpec(memory_space=pltpu.VMEM)
SMEM = pl.BlockSpec(memory_space=pltpu.SMEM)


def call(body, out_shape, n_smem, n_vmem, us, scratch=(), vmem=16):
    return pl.pallas_call(
        body,
        out_shape=out_shape,
        in_specs=[SMEM] * n_smem + [VMEM] * n_vmem,
        out_specs=jax.tree.map(lambda _: VMEM, out_shape),
        scratch_shapes=list(scratch),
        name=getattr(body, "func", body).__name__,
        compiler_params=pltpu.CompilerParams(vmem_limit_bytes=vmem * 2**20),
        cost_estimate=pl.CostEstimate(
            flops=int(us * 1.1e9 * COST), bytes_accessed=int(us * 3e6 * COST), transcendentals=0
        ),
    )


def dot(a, b, contract=(1, 0)):
    return lax.dot_general(
        a, b, (((contract[0],), (contract[1],)), ((), ())), preferred_element_type=F32
    )


def iota(shape, axis):
    return lax.broadcasted_iota(jnp.int32, shape, axis)


def head_groups(ids, q_ref, k_ref, v_ref, *outs):
    for i, out in enumerate(outs):
        cols = pl.ds(pl.multiple_of((ids[0] ^ i) * GROUP, 128), GROUP)
        for t, ref in enumerate((q_ref, k_ref, v_ref)):
            out[t] = ref[:, cols]


STATE = (
    jax.ShapeDtypeStruct((2, 8, 2 * TOKENS), F32),
    jax.ShapeDtypeStruct((2, 8, 2 * TOKENS), F32),
    jax.ShapeDtypeStruct((2, HEADS // 4, HEAD_DIM, 2 * TOKENS), F32),
)


def absorb(ids, mask_ref, q_ref, u, sources, state):
    group, place = ids[0], ids[1]
    half, core = group // 2, group % 2
    lanes = iota((1, 2 * TOKENS), 1)
    biases = []
    for _, half_k, place_k in sources:
        for j in range(2):
            frame_k = 16 * half_k + 2 * place_k + (core ^ j)
            seen = [
                jnp.where(mask_ref[16 * (half ^ u) + 2 * place + (core ^ a), frame_k] > 0, 0.0, FLOOR)
                for a in range(2)
            ]
            biases.append(jnp.where(lanes < TOKENS, seen[0], seen[1]).astype(F32))
    new = []
    for h in range(GROUP // HEAD_DIM):
        cols = slice(h * HEAD_DIM, (h + 1) * HEAD_DIM)
        q = q_ref[u, :, :, cols].reshape(2 * TOKENS, HEAD_DIM)
        k = jnp.concatenate([load(0, cols) for load, _, _ in sources], axis=0)
        v = jnp.concatenate([load(1, cols) for load, _, _ in sources], axis=0)
        scores = dot(k, q, (1, 1))
        parts = [scores[i * TOKENS : (i + 1) * TOKENS] for i in range(len(biases))]
        tops = [
            jnp.max(s, axis=0, keepdims=True) * LOG2_SCALE + bias for s, bias in zip(parts, biases)
        ]
        top = functools.reduce(jnp.maximum, tops)
        if state is not None:
            old, total_in, acc_in = state[h]
            top = jnp.maximum(top, old)
        probs = [jnp.exp2(s * LOG2_SCALE + (bias - top)) for s, bias in zip(parts, biases)]
        pb = jnp.concatenate([p.astype(BF16) for p in probs], axis=0); total = dot(jnp.ones((8, pb.shape[0]), BF16), pb)[:1]
        update = dot(v, pb, (0, 0))
        if state is not None:
            factor = jnp.exp2(old - top)
            total = total_in * factor + total
            update = acc_in * factor + update
        new.append((top, total, update))
    return new


def loader(ref):
    return lambda t, cols: ref[:, t, :, cols].reshape(2 * TOKENS, HEAD_DIM)


def either(first, a_ref, b_ref):
    a, b = loader(a_ref), loader(b_ref)
    return lambda t, cols: jnp.where(first, a(t, cols), b(t, cols))


def read_state(u, m_ref, l_ref, acc_ref):
    return [
        (m_ref[u, h : h + 1, :], l_ref[u, h : h + 1, :], acc_ref[u, h])
        for h in range(GROUP // HEAD_DIM)
    ]


def write_state(u, new, m_ref, l_ref, acc_ref):
    for h, (top, total, acc) in enumerate(new):
        m_ref[u, h : h + 1, :] = top
        l_ref[u, h : h + 1, :] = total
        acc_ref[u, h] = acc
    rest = jnp.zeros((8 - len(new), 2 * TOKENS), F32)
    m_ref[u, len(new) :, :] = rest
    l_ref[u, len(new) :, :] = rest


def attend_own(ids, mask_ref, own, core, other, both, m_ref, l_ref, acc_ref, q_out):
    half = ids[0] // 2
    for u, pair in enumerate(((own, core), (other, both))):
        q_out[u, 0], q_out[u, 1] = pair[0][0], pair[1][0]
    for u, (first, second) in enumerate(((own, core), (other, both))):

        def load(t, cols):
            return jnp.concatenate([first[t + 1, :, cols], second[t + 1, :, cols]], axis=0)

        new = absorb(ids, mask_ref, q_out, u, [(load, half ^ u, ids[1])], None)
        write_state(u, new, m_ref, l_ref, acc_ref)


def attend_step(step, ids, mask_ref, q_ref, a_up, a_down, b_up, b_down, *states):
    half, place = ids[0] // 2, ids[1]
    above, below = place + step, place - step
    for u in range(2):
        flip_up, flip_down = u ^ (above // 8), u ^ jnp.where(below < 0, 1, 0)
        sources = [
            (either(flip_up == 0, a_up, b_up), half ^ flip_up, above % 8),
            (either(flip_down == 0, a_down, b_down), half ^ flip_down, (below + 8) % 8),
        ]
        new = absorb(ids, mask_ref, q_ref, u, sources, read_state(u, *states[:3]))
        write_state(u, new, *states[3:])


def attend_last(u, ids, mask_ref, q_ref, a_ref, b_ref, m_in, l_in, acc_in, *outs):
    half, far = ids[0] // 2, (ids[1] + 4) % 8
    sources = [(loader(a_ref), half, far), (loader(b_ref), half ^ 1, far)]
    state = read_state(u, m_in, l_in, acc_in)
    for h, (_, total, acc) in enumerate(absorb(ids, mask_ref, q_ref, u, sources, state)):
        out = (acc / total).T.astype(BF16)
        cols = slice(h * HEAD_DIM, (h + 1) * HEAD_DIM)
        outs[0][:, cols] = out[:TOKENS]
        outs[1][:, cols] = out[TOKENS:]


def scan_pack(x_ref, bc_ref, log_ref, out_ref):
    lanes = iota((TOKENS, 128), 1)
    logs = log_ref[...].astype(F32)
    turned = pltpu.roll(logs, 64, 1)
    bc = bc_ref[...]
    for s in range(N_SPACE):
        base = 384 * (s // 2) + 128 * (s % 2)
        out_ref[s, :, :WIN] = x_ref[:, base : base + WIN]
        out_ref[s, :, WIN:] = bc
        heads, spun = logs[3 * s : 3 * s + 3], turned[3 * s : 3 * s + 3]
        rows = [heads, spun] if s % 2 else [spun, heads]
        rows = jnp.concatenate(rows + [jnp.zeros((10, 128), F32)], axis=0)
        at = slice(0, 128) if s % 2 else slice(128, 256)
        free = lanes[:16] < 64 if s % 2 else lanes[:16] >= 64
        out_ref[s, :16, at] = jnp.where(free, rows, out_ref[s, :16, at].astype(F32)).astype(BF16)


def split_high(a):
    high = a.astype(BF16)
    return high, (a - high.astype(F32)).astype(BF16)


def ones_where(condition):
    return jnp.where(condition, 1.0, 0.0).astype(BF16)


def log_rows(in_ref, odd):
    low = iota((8, 128), 1) < 64
    keep = iota((8, 128), 0) < 3
    tiles = []
    for s in range(N_SPACE):
        left, right = in_ref[s, :16, :128].astype(F32)[:8], in_ref[s, :16, 128:WIN].astype(F32)[:8]
        first = jnp.where(odd == 1, left, pltpu.roll(right, 64, 1))
        second = pltpu.roll(first, 64, 1)
        second = jnp.concatenate([second[3:], second[:3]], axis=0)
        tiles.append(jnp.where(keep, jnp.where(low, first, second), 0.0))
    return jnp.concatenate(tiles, axis=0).astype(BF16)


def stacked(rows, weights):
    out = dot(rows, weights)
    return [out[8 * s : 8 * s + 8] for s in range(N_SPACE)]


def running(parts):
    sums = [jnp.zeros_like(parts[0])]
    for part in parts:
        sums.append(sums[-1] + part)
    return sums[:-1], sums[-1]


def heads_diagonal(blocks, group, odd):
    return functools.reduce(
        jnp.add, [jnp.where(group == h + odd, block, 0.0) for h, block in enumerate(blocks)]
    )


def scan_state(ids, order_ref, in_ref, row_ref, col_ref, state_ref, sent_ref):
    odd = ids[2] % 2
    logs = log_rows(in_ref, odd)
    i, j = iota((TOKENS, TOKENS), 0), iota((TOKENS, TOKENS), 1)
    every = jnp.ones((TOKENS, TOKENS), BF16)
    row_before, total = running(stacked(logs, every))
    row_cum = [a + b for a, b in zip(stacked(logs, ones_where(i <= j)), row_before)]

    rank = jnp.zeros((TOKENS, TOKENS), F32)
    for k in range(COLS):
        rank = jnp.where(j % COLS == order_ref[k], float(k), rank)
    same_col = i % COLS == j % COLS
    earlier = stacked(logs, ones_where(rank.T < rank))
    earlier = functools.reduce(jnp.add, earlier)
    col_before, _ = running(stacked(logs, ones_where(same_col)))
    within = stacked(logs, ones_where(same_col & (i <= j)))
    col_cum = [a + b + earlier for a, b in zip(within, col_before)]

    group = iota((STATE_DIM, WIN), 1) // 64
    state = [jnp.zeros((STATE_DIM, WIN), F32)] * 6
    for s in range(N_SPACE):
        row_ref[s], col_ref[s] = row_cum[s], col_cum[s]
        b_turned = in_ref[s, :, WIN:].astype(F32).T[:STATE_DIM]
        lhs = []
        for cum in (row_cum[s], col_cum[s]):
            kept = jnp.exp(total - cum)
            lhs += [(b_turned * kept[h : h + 1]).astype(BF16) for h in range(3)]
        out = dot(jnp.concatenate(lhs, axis=0), in_ref[s, :, :WIN])
        state = [a + out[STATE_DIM * n : STATE_DIM * (n + 1)] for n, a in enumerate(state)]
    wide = jnp.concatenate([total, total], axis=1)
    lane_total = heads_diagonal(
        [jnp.broadcast_to(wide[h : h + 1], (8, WIN)) for h in range(3)], group[:8], odd
    )
    for n in range(2):
        at = n * ROWS
        own = heads_diagonal(state[3 * n : 3 * n + 3], group, odd)
        own = jnp.concatenate([own, lane_total], axis=0)
        state_ref[at : at + ROWS, :] = own
        sent_ref[n] = to_send(own)


def scan_inside(by_column, ids, order_ref, in_ref, *rest):
    odd = ids[2] % 2
    y_ref, buf = rest

    def strided(s, t):
        return in_ref[s, :, t * 128 : (t + 1) * 128].astype(F32)

    if by_column:
        rows, buf = buf.at[0], buf.at[1]
        for s in range(N_SPACE):
            for t in range(3):
                rows[t, s * TOKENS : (s + 1) * TOKENS, :] = strided(s, t)
        for k in range(COLS):
            for t in range(3):
                buf[t, k * 32 : (k + 1) * 32, :] = rows[t, pl.ds(order_ref[k], 32, stride=COLS), :]

    def load(b, t):
        return buf[t, b * TOKENS : (b + 1) * TOKENS, :] if by_column else strided(b, t)

    i, j = iota((TOKENS, TOKENS), 0), iota((TOKENS, TOKENS), 1)
    lower_mask = i >= j
    upper = ones_where(i <= j)
    every = jnp.ones((TOKENS, TOKENS), BF16)
    logs = log_rows(in_ref, odd)
    tile_of = (iota((8, TOKENS), 1) % 32) // 4
    col_logs = []
    for b in range(N_SPACE) if by_column else ():
        column = jnp.zeros((TOKENS, TOKENS), jnp.int32)
        for k in range(4):
            column = jnp.where(j // 32 == k, order_ref[4 * b + k], column)
        picked = stacked(logs, ones_where((i % COLS == column) & (i // COLS == j % 4)))
        log = jnp.zeros((8, TOKENS), F32)
        for s in range(N_SPACE):
            log = jnp.where(tile_of == s, picked[s], log)
        col_logs.append(log)
    if by_column:
        logs = jnp.concatenate(col_logs, axis=0).astype(BF16)

    group = iota((TOKENS, WIN), 1) // 64
    state_group = iota((STATE_DIM, WIN), 1) // 64

    def write_row(b, out):
        for t in range(2):
            y_ref[t, b * TOKENS : (b + 1) * TOKENS, :] = out[:, t * 128 : (t + 1) * 128]

    def write_col(b, out):
        for k in range(TOKENS // 32):
            here = pl.ds(order_ref[b * 4 + k], 32, stride=COLS)
            for t in range(2):
                part = out[k * 32 : (k + 1) * 32, t * 128 : (t + 1) * 128]
                y_ref[t, here, :] = part

    write = write_col if by_column else write_row
    carry = None
    cums, totals = stacked(logs, upper), stacked(logs, every)
    for b in range(N_SPACE):
        window = jnp.concatenate([load(b, 0), load(b, 1)], axis=1)
        bc = load(b, 2)
        turned, bc = bc.T, bc.astype(BF16)
        b_turned, c_turned = turned[:STATE_DIM], turned[STATE_DIM:]
        scores = dot(bc[:, STATE_DIM:], bc[:, :STATE_DIM], (1, 1))
        cum = cums[b]
        lhs, rhs = [], []
        for h in range(3):
            cum_j = jnp.broadcast_to(cum[h : h + 1], (TOKENS, TOKENS))
            gap = jnp.where(lower_mask, cum_j.T - cum_j, FLOOR)
            lhs.append((scores * jnp.exp(gap)).astype(BF16))
            rhs.append(jnp.where(group == h + odd, window, 0.0).astype(BF16))
        if carry is not None:
            decay = jnp.exp(cum)
            scaled = [c_turned * decay[h : h + 1] for h in range(3)]
            scaled.append(jnp.zeros_like(c_turned))
            scaled = jnp.concatenate(scaled, axis=0)
            lhs += [scaled[:128].T.astype(BF16), scaled[128:].T.astype(BF16)]
            for h in range(3):
                rhs.append(jnp.where(state_group == h + odd, carry[h], 0.0).astype(BF16))
            rhs.append(jnp.zeros((STATE_DIM, WIN), BF16))
        write(b, dot(jnp.concatenate(lhs, axis=1), jnp.concatenate(rhs, axis=0)))
        if b < N_SPACE - 1:
            kept = jnp.exp(totals[b] - cum)
            kept = [(b_turned * kept[h : h + 1]).astype(BF16) for h in range(3)]
            local = dot(jnp.concatenate(kept, axis=0), window.astype(BF16))
            local = [local[STATE_DIM * h : STATE_DIM * (h + 1)] for h in range(3)]
            if carry is not None:
                fade = jnp.exp(totals[b])
                fade = jnp.concatenate([fade, fade], axis=1)
                local = [a + fade[h : h + 1] * c for h, (a, c) in enumerate(zip(local, carry))]
            carry = local


def scan_finish(
    ids, in_ref, y_ref, z_ref, row_ref, col_ref, before_ref, swapped_ref, core_ref, gain_ref, out_ref
):
    odd = ids[2] % 2
    same = ones_where(iota((WIN, WIN), 0) // 64 == iota((WIN, WIN), 1) // 64)
    group = iota((STATE_DIM, WIN), 1) // 64
    core = ids[0] % 2
    states = []
    for n in range(2):
        state = jnp.where(core == n, before_ref[...].astype(F32), swapped_ref[...].astype(F32))
        first = from_sent(core_ref[n])
        decay = jnp.exp(first[STATE_DIM : STATE_DIM + 1])
        state = jnp.where(core == 1, decay * state + first[:STATE_DIM], state)
        states += [jnp.where(group == h + odd, state, 0.0).astype(BF16) for h in range(3)]
    states = jnp.concatenate(states, axis=0)
    gain = gain_ref[...]
    for s in range(N_SPACE):
        here = slice(s * TOKENS, (s + 1) * TOKENS)
        c_turned = in_ref[s, :, WIN:].astype(F32).T[STATE_DIM:]
        scaled = []
        for ref in (row_ref, col_ref):
            decay = jnp.exp(ref[s])
            scaled += [c_turned * decay[h : h + 1] for h in range(3)]
        scaled = [
            jnp.concatenate(scaled[2 * n : 2 * n + 2], axis=0).T.astype(BF16) for n in range(3)
        ]
        total = jnp.concatenate([y_ref[t, here, :] + z_ref[t, here, :] for t in range(2)], axis=1)
        total = total + dot(jnp.concatenate(scaled, axis=1), states)
        meansq = dot((total * total).astype(BF16), same) * (1.0 / SCAN_DIM)
        normed = total * lax.rsqrt(meansq + EPS) * gain
        left, right = normed[:, :128], normed[:, 128:]
        full = jnp.where(odd == 1, right, left)
        part = jnp.where(odd == 1, left, right)
        out_ref[s, :TOKENS, :] = full.astype(BF16)
        out_ref[s, TOKENS:, :] = (part[:64] + pltpu.roll(part[64:], 64, 1)).astype(BF16)


SENT = STATE_DIM + 16


def to_send(state):
    high, low = split_high(state[STATE_DIM:])
    return jnp.concatenate([state[:STATE_DIM].astype(BF16), high, low], axis=0)


def from_sent(sent):
    sent = sent.astype(F32)
    decay = sent[STATE_DIM : STATE_DIM + 8] + sent[STATE_DIM + 8 :]
    return jnp.concatenate([sent[:STATE_DIM], decay], axis=0)


def join(earlier, later):
    decay = jnp.exp(later[STATE_DIM : STATE_DIM + 1])
    return jnp.where(iota((ROWS, WIN), 0) < STATE_DIM, decay, 1.0) * earlier + later


def chip_state(ids, own_ref, got_ref, total_ref, sent_ref):
    core = ids[0] % 2
    at = pl.ds(pl.multiple_of(core * ROWS, 8), ROWS)
    own, other = own_ref[at, :], from_sent(got_ref[core])
    first = core == 0
    total = join(jnp.where(first, own, other), jnp.where(first, other, own))
    total_ref[...] = total
    sent_ref[...] = to_send(total)


def grow(bit, ids, got_ref, total_in, *rest):
    before_in, (before_ref, total_ref, sent_ref) = (rest[0], rest[1:]) if bit > 2 else (None, rest)
    other, total = from_sent(got_ref[...]), total_in[...]
    later = (ids[3] & bit) > 0
    before = other if before_in is None else join(other, before_in[...])
    before_ref[...] = jnp.where(later, before, 0.0 if before_in is None else before_in[...])
    total = join(jnp.where(later, other, total), jnp.where(later, total, other))
    total_ref[...] = total
    sent_ref[...] = to_send(total)


def last_before(ids, got_ref, before_in, sent_ref):
    before = before_in[...]
    before = jnp.where((ids[3] & 16) > 0, join(from_sent(got_ref[...]), before), before)
    sent_ref[...] = before[:STATE_DIM].astype(BF16)


def add_up(ids, scan_ref, *rest):
    group = ids[0]
    out_ref, total = rest[4], rest[5]
    low_half = iota((64, 128), 1) < 64
    for k in range(4):
        even, uneven = scan_ref[2 * k], scan_ref[2 * k + 1]
        e, o = even[TOKENS:].astype(F32), uneven[TOKENS:].astype(F32)
        total[:, 384 * k : 384 * k + 128] = even[:TOKENS].astype(F32)
        total[:64, 384 * k + 128 : 384 * k + 256] = jnp.where(low_half, e, o)
        total[64:, 384 * k + 128 : 384 * k + 256] = jnp.where(
            low_half, pltpu.roll(e, 64, 1), pltpu.roll(o, 64, 1)
        )
        total[:, 384 * k + 256 : 384 * k + 384] = uneven[:TOKENS].astype(F32)
    for i in range(4):
        cols = pl.ds(pl.multiple_of((group ^ i) * GROUP, 128), GROUP)
        out_ref[:, cols] = (total[:, cols] + rest[i][...].astype(F32)).astype(BF16)


def tie(*values):
    return lax.optimization_barrier(values)


def z_shift(array, by):
    pairs = []
    for half in range(2):
        for z in range(8):
            for core in range(2):
                pairs.append((16 * half + 2 * z + core, 16 * half + 2 * ((z + by) % 8) + core))
    return lax.ppermute(array, "tm", pairs)


def partner(array, bits):
    return lax.ppermute(array, "tm", [(i, i ^ bits) for i in range(N_TM)])


def on_device(queries, keys, values, tile_mask, inner_x, bc_proj, log_decay, col_order, norm_gain):
    frame = lax.axis_index("tm")
    tile = lax.axis_index("space")
    group = 2 * (frame // 16) + frame % 2
    ids = jnp.stack([group, (frame // 2) % 8, tile, frame]).astype(jnp.int32)

    qkv = jax.ShapeDtypeStruct((3, TOKENS, GROUP), BF16)
    own, to_core, to_half, to_both = call(
        head_groups, (qkv,) * 4, 1, 3, 1, vmem=56
    )(ids, queries, keys, values)
    from_core = partner(to_core, 1)
    from_half = partner(to_half, 16)
    from_both = partner(to_both, 17)
    chunks = {(0, 0): jnp.stack([own[1:], from_core[1:]])}
    inner_x, _ = tie(inner_x, chunks[0, 0])
    sent = call(
        scan_pack, jax.ShapeDtypeStruct((N_SPACE, TOKENS, WIN + 128), BF16), 0, 3, 1.5, vmem=56
    )(inner_x, bc_proj, log_decay)
    frame_in = lax.all_to_all(sent, "space", split_axis=0, concat_axis=0, tiled=True)


    def pass_on(source, step, after=None):
        if after is not None:
            behind, _ = tie(pair(source, step - 1), after)
            chunks[source, step - 1], chunks[source, 1 - step] = behind
        for sign in (1, -1):
            chunks[source, sign * step] = z_shift(chunks[source, sign * (step - 1)], -sign)

    def pair(source, step):
        return chunks[source, step], chunks[source, -step]

    def step_of(step, flash):
        return call(functools.partial(attend_step, step), STATE, 2, 8, 2.5)(
            ids, tile_mask, q_all, *pair(0, step), *pair(1, step), *flash
        )

    pass_on(0, 1)
    pass_on(0, 2)
    chunks[1, 0] = jnp.stack([from_half[1:], from_both[1:]])
    pass_on(1, 1)
    cum = jax.ShapeDtypeStruct((N_SPACE, 8, TOKENS), F32)
    one, sent = jax.ShapeDtypeStruct((ROWS, WIN), F32), jax.ShapeDtypeStruct((SENT, WIN), BF16)
    row_cum, col_cum, state, both_sent = call(
        scan_state,
        (
            cum,
            cum,
            jax.ShapeDtypeStruct((2 * ROWS, WIN), F32),
            jax.ShapeDtypeStruct((2, SENT, WIN), BF16),
        ),
        2,
        1,
        2,
    )(ids, col_order, frame_in)
    core_sent = partner(both_sent, 1)
    total, walk = call(chip_state, (one, sent), 1, 2, 0.5)(ids, state, core_sent)

    other = partner(walk, 2)
    own, _ = tie(own, walk)
    *flash, q_all = call(
        attend_own, STATE + (jax.ShapeDtypeStruct((2, 2, TOKENS, GROUP), BF16),), 2, 4, 2
    )(ids, tile_mask, own, from_core, from_half, from_both)
    other, flash = tie(other, flash)
    before, total, walk = call(functools.partial(grow, 2), (one, one, sent), 1, 2, 0.5)(
        ids, other, total
    )

    other = partner(walk, 4)
    frame_tokens = N_SPACE * TOKENS
    wide = jax.ShapeDtypeStruct((2, frame_tokens, 128), F32)
    pass_on(0, 3, walk)
    inside_in, _ = tie(frame_in, pair(1, 1))
    y_row = call(
        functools.partial(scan_inside, False), wide, 2, 1, 2, [pltpu.VMEM((8, 128), F32)]
    )(ids, col_order, inside_in)
    pass_on(1, 2, y_row)
    flash, y_row = tie(flash, y_row)
    flash = step_of(1, flash)
    other, flash, y_row = tie(other, flash, y_row)
    before, total, walk = call(functools.partial(grow, 4), (one, one, sent), 1, 3, 0.5)(
        ids, other, total, before
    )

    other = partner(walk, 8)
    pass_on(1, 3, walk)
    inside_in, _, _ = tie(inside_in, walk, pair(0, 3))
    y_col = call(
        functools.partial(scan_inside, True),
        wide,
        2,
        1,
        4,
        [pltpu.VMEM((2, 3, frame_tokens, 128), F32)],
    )(ids, col_order, inside_in)
    flash, y_col = tie(flash, y_col)
    flash = step_of(2, flash)
    other, flash, y_col = tie(other, flash, y_col)
    before, total, walk = call(functools.partial(grow, 8), (one, one, sent), 1, 3, 0.5)(
        ids, other, total, before
    )

    other = partner(walk, 16)
    (to_up, to_down), flash, walk = tie((chunks[0, 3], chunks[1, -3]), flash, walk)
    far_a, far_b = z_shift(to_up, -1), z_shift(to_down, 1)
    flash = step_of(3, flash)
    other, flash = tie(other, flash)
    before = call(last_before, jax.ShapeDtypeStruct((STATE_DIM, WIN), BF16), 1, 2, 0.5)(
        ids, other, before
    )
    before_other = partner(before, 1)

    gain = lax.dynamic_slice(norm_gain, (384 * (tile // 2) + 128 * (tile % 2),), (WIN,))
    normed = call(scan_finish, jax.ShapeDtypeStruct((N_SPACE, 192, 128), BF16), 1, 9, 3)(
        ids,
        frame_in,
        y_row,
        y_col,
        row_cum,
        col_cum,
        before,
        before_other,
        core_sent,
        gain.reshape(1, WIN),
    )
    scan_rows = lax.all_to_all(normed, "space", split_axis=0, concat_axis=0, tiled=True)
    flash, _ = tie(flash, normed)
    piece = jax.ShapeDtypeStruct((TOKENS, GROUP), BF16)
    pieces = {}
    for u in (1, 0):
        pieces[u] = call(functools.partial(attend_last, u), (piece, piece), 2, 6, 2)(
            ids, tile_mask, q_all, far_a, far_b, *flash
        )
        flash, pieces[u] = tie(flash, pieces[u])
    attention = (
        pieces[0][0],
        partner(pieces[0][1], 1),
        partner(pieces[1][0], 16),
        partner(pieces[1][1], 17),
    )
    return call(
        add_up,
        jax.ShapeDtypeStruct((TOKENS, HEADS * HEAD_DIM), BF16),
        1,
        5,
        1.5,
        [pltpu.VMEM((TOKENS, HEADS * HEAD_DIM), F32)],
    )(ids, scan_rows, *attention)


def solution(mesh):
    return jax.shard_map(
        on_device,
        mesh=mesh,
        in_specs=(
            P(("tm", "space"), None),
            P(("tm", "space"), None),
            P(("tm", "space"), None),
            P(),
            P(("tm", "space"), None),
            P(("tm", "space"), None),
            P(None, ("tm", "space")),
            P(),
            P(),
        ),
        out_specs=P(("tm", "space"), None),
        check_vma=False,
    )
```

profile of v0, /device:TPU:1, one launch (start us, length us, event | category | flops | bytes accessed | tf_op | source)
XLA Modules:
  0.0 118.0 jit_solution(3160488937759009906)
XLA Ops:
  0.0 0.6 pad_add_fusion.ids
  0.6 2.4 %head_groups.1 = (bf16[3,128,384]{2,1,0:T(8,128)(2,1)}, bf16[3,128,384]{2,1,0:T(8,128)(2,1)}, bf16[3,128,384]{2,1,0:T(8,128)(2,1)}, bf16[3,128,384]{2,1,0:T(8,128)(2,1)}) custom-call(s32[4]{0:T(128)} %pad_add_fusion.ids, bf16[128,1536]{1,0:T(8,128)(2,1)} %q_ref.1, bf16[128,1536]{1,0:T(8,128)(2,1)} %k_ref.1, bf16[128,1536]{1,0:T(8,128)(2,1)} %v_ref.1), custom_call_target="tpu_custom_call" | custom-call | flops 110000000 | bytes 300000 | tf_op jit(solution)/shard_map/head_groups/pallas_call | solution.py:489
  2.9 3.2 %collective-permute-start = (bf16[3,128,384]{2,1,0:T(8,128)(2,1)}, bf16[3,128,384]{2,1,0:T(8,128)(2,1)S(1)}, u32[]{:S(2)}, u32[]{:S(2)}) collective-permute-start(bf16[3,128,384]{2,1,0:T(8,128)(2,1)} %get-tuple-element.92), channel_id=1, source_target_pairs={{0,8},{8,0},{16,24},{24,16},{32,40},{40,32},{48,56},{56,48},{64,72... | collective-permute-start | bytes 884744 | tf_op jit(solution)/shard_map/ppermute | solution.py:479
  6.2 1.0 collective-permute-start.3
  7.2 2.1 %collective-permute-start.4 = (bf16[3,128,384]{2,1,0:T(8,128)(2,1)}, bf16[3,128,384]{2,1,0:T(8,128)(2,1)S(1)}, u32[]{:S(2)}, u32[]{:S(2)}) collective-permute-start(bf16[3,128,384]{2,1,0:T(8,128)(2,1)} %get-tuple-element.99), channel_id=1, source_target_pairs={{0,136},{8,128},{16,152},{24,144},{32,168},{40,160},{48,184},{56,1... | collective-permute-start | bytes 884744 | tf_op jit(solution)/shard_map/ppermute | solution.py:479
  9.3 0.9 slice_bitcast_fusion.3
  10.4 3.9 %collective-permute-start.6 = (bf16[2,2,128,384]{3,2,1,0:T(8,128)(2,1)S(1)}, bf16[2,2,128,384]{3,2,1,0:T(8,128)(2,1)}, u32[]{:S(2)}, u32[]{:S(2)}) collective-permute-start(bf16[2,2,128,384]{3,2,1,0:T(8,128)(2,1)S(1)} %pad_maximum_fusion), channel_id=1, source_target_pairs={{0,112},{8,120},{16,0},{24,8},{32,16},{40,24},{48,32},{56,40},{64,... | collective-permute-start | bytes 1179656 | tf_op jit(solution)/shard_map/ppermute | solution.py:475
  14.3 2.0 %scan_pack.1 = bf16[8,128,384]{2,1,0:T(8,128)(2,1)} custom-call(bf16[128,1536]{1,0:T(8,128)(2,1)} %x_ref, bf16[128,128]{1,0:T(8,128)(2,1)} %bc_ref.1, bf16[24,128]{1,0:T(8,128)(2,1)} %log_ref.1), custom_call_target="tpu_custom_call" | custom-call | flops 165000000 | bytes 450000 | tf_op jit(solution)/shard_map/scan_pack/pallas_call | solution.py:497
  16.3 5.1 %all-to-all-start = ((bf16[8,128,384]{2,1,0:T(8,128)(2,1)}), bf16[8,128,384]{2,1,0:T(8,128)(2,1)S(1)}, u32[]{:S(2)}, u32[]{:S(2)}) async-start(bf16[8,128,384]{2,1,0:T(8,128)(2,1)} %scan_pack.1), calls=%async_computation | async-start | bytes 1572864 | tf_op jit(solution)/shard_map/all_to_all | solution.py:500
  21.4 1.5 %collective-permute-done.4.both = bf16[3,128,384]{2,1,0:T(8,128)(2,1)S(1)} collective-permute-done((bf16[3,128,384]{2,1,0:T(8,128)(2,1)}, bf16[3,128,384]{2,1,0:T(8,128)(2,1)S(1)}, u32[]{:S(2)}, u32[]{:S(2)}) %collective-permute-start.4) | collective-permute-done | bytes 294944 | tf_op jit(solution)/shard_map/ppermute | solution.py:479
  23.1 3.9 %collective-permute-start.8 = (bf16[2,2,128,384]{3,2,1,0:T(8,128)(2,1)S(1)}, bf16[2,2,128,384]{3,2,1,0:T(8,128)(2,1)}, u32[]{:S(2)}, u32[]{:S(2)}) collective-permute-start(bf16[2,2,128,384]{3,2,1,0:T(8,128)(2,1)S(1)} %pad_maximum_fusion.1), channel_id=1, source_target_pairs={{0,112},{8,120},{16,0},{24,8},{32,16},{40,24},{48,32},{56,40},{64,... | collective-permute-start | bytes 1179656 | tf_op jit(solution)/shard_map/ppermute | solution.py:475
  27.0 2.7 %collective-permute-start.11 = (bf16[2,2,128,384]{3,2,1,0:T(8,128)(2,1)}, bf16[2,2,128,384]{3,2,1,0:T(8,128)(2,1)}, u32[]{:S(2)}, u32[]{:S(2)}) collective-permute-start(bf16[2,2,128,384]{3,2,1,0:T(8,128)(2,1)} %collective-permute-done.6.a_up), channel_id=1, source_target_pairs={{0,112},{8,120},{16,0},{24,8},{32,16},{40,24},{48,32},{56,40},{64,... | collective-permute-start | bytes 1179656 | tf_op jit(solution)/shard_map/ppermute | solution.py:475
  29.7 5.5 %collective-permute-done.8.b_up = bf16[2,2,128,384]{3,2,1,0:T(8,128)(2,1)} collective-permute-done((bf16[2,2,128,384]{3,2,1,0:T(8,128)(2,1)S(1)}, bf16[2,2,128,384]{3,2,1,0:T(8,128)(2,1)}, u32[]{:S(2)}, u32[]{:S(2)}) %collective-permute-start.8) | collective-permute-done | bytes 393248 | tf_op jit(solution)/shard_map/ppermute | solution.py:475
  35.2 3.2 %collective-permute-done.9.b_down = bf16[2,2,128,384]{3,2,1,0:T(8,128)(2,1)} collective-permute-done((bf16[2,2,128,384]{3,2,1,0:T(8,128)(2,1)S(1)}, bf16[2,2,128,384]{3,2,1,0:T(8,128)(2,1)}, u32[]{:S(2)}, u32[]{:S(2)}) %collective-permute-start.9) | collective-permute-done | bytes 393248 | tf_op jit(solution)/shard_map/ppermute | solution.py:475
  38.4 2.2 %scan_inside.2.y_ref = f32[2,1024,128]{2,1,0:T(8,128)S(1)} custom-call(s32[4]{0:T(128)S(1)} %copy-done.5, s32[32]{0:T(128)S(1)} %copy-done.6, bf16[8,128,384]{2,1,0:T(8,128)(2,1)S(1)} %all-to-all-done.in_ref), custom_call_target="tpu_custom_call" | custom-call | flops 220000000 | bytes 600000 | tf_op jit(solution)/shard_map/scan_inside/pallas_call | solution.py:554
  41.0 1.1 collective-permute-start.14
  42.2 1.4 %scan_state.1 = (f32[8,8,128]{2,1,0:T(8,128)S(1)}, f32[8,8,128]{2,1,0:T(8,128)S(1)}, f32[144,256]{1,0:T(8,128)S(1)}, bf16[2,80,256]{2,1,0:T(8,128)(2,1)S(1)}) custom-call(s32[4]{0:T(128)S(1)} %copy-done.5, s32[32]{0:T(128)S(1)} %copy-done.6, bf16[8,128,384]{2,1,0:T(8,128)(2,1)S(1)} %all-to-all-done.in_ref), custom_call_target="tpu_custom_call" | custom-call | flops 220000000 | bytes 600000 | tf_op jit(solution)/shard_map/scan_state/pallas_call | solution.py:524
  43.6 3.1 %collective-permute-start.1 = (bf16[2,80,256]{2,1,0:T(8,128)(2,1)S(1)}, bf16[2,80,256]{2,1,0:T(8,128)(2,1)S(1)}, u32[]{:S(2)}, u32[]{:S(2)}) collective-permute-start(bf16[2,80,256]{2,1,0:T(8,128)(2,1)S(1)} %get-tuple-element.95), channel_id=1, source_target_pairs={{0,8},{8,0},{16,24},{24,16},{32,40},{40,32},{48,56},{56,48},{64,72... | collective-permute-start | bytes 245768 | tf_op jit(solution)/shard_map/ppermute | solution.py:479
  46.7 0.9 collective-permute-done.1.got_ref.core_ref
  47.6 0.6 chip_state.1
  48.5 1.7 %attend_own.1 = (f32[2,8,256]{2,1,0:T(8,128)S(1)}, f32[2,8,256]{2,1,0:T(8,128)S(1)}, f32[2,3,128,256]{3,2,1,0:T(8,128)S(1)}, bf16[2,2,128,384]{3,2,1,0:T(8,128)(2,1)S(1)}) custom-call(s32[4]{0:T(128)S(1)} %copy-done.5, s32[32,32]{1,0:T(8,128)S(1)} %copy-done.4, bf16[3,128,384]{2,1,0:T(8,128)(2,1)S(1)} %copy-done.3, ...), custom_call_target="tpu_custom_call" | custom-call | flops 220000000 | bytes 600000 | tf_op jit(solution)/shard_map/attend_own/pallas_call | solution.py:541
  50.2 2.0 %collective-permute-done.2.got_ref = bf16[80,256]{1,0:T(8,128)(2,1)S(1)} collective-permute-done((bf16[80,256]{1,0:T(8,128)(2,1)S(1)}, bf16[80,256]{1,0:T(8,128)(2,1)S(1)}, u32[]{:S(2)}, u32[]{:S(2)}) %collective-permute-start.2) | collective-permute-done | bytes 40992 | tf_op jit(solution)/shard_map/ppermute | solution.py:479
  52.7 4.1 %collective-permute-start.15 = (bf16[2,2,128,384]{3,2,1,0:T(8,128)(2,1)}, bf16[2,2,128,384]{3,2,1,0:T(8,128)(2,1)}, u32[]{:S(2)}, u32[]{:S(2)}) collective-permute-start(bf16[2,2,128,384]{3,2,1,0:T(8,128)(2,1)} %collective-permute-done.11.a_up), channel_id=1, source_target_pairs={{0,112},{8,120},{16,0},{24,8},{32,16},{40,24},{48,32},{56,40},{64,... | collective-permute-start | bytes 1179656 | tf_op jit(solution)/shard_map/ppermute | solution.py:475
  56.8 2.8 %attend_step.3 = (f32[2,8,256]{2,1,0:T(8,128)S(1)}, f32[2,8,256]{2,1,0:T(8,128)S(1)}, f32[2,3,128,256]{3,2,1,0:T(8,128)S(1)}) custom-call(s32[4]{0:T(128)S(1)} %copy-done.5, s32[32,32]{1,0:T(8,128)S(1)} %copy-done.4, bf16[2,2,128,384]{3,2,1,0:T(8,128)(2,1)S(1)} %get-tuple-element.106.q_ref, bf16[2,2,128,384]{3,2,1,0:T(8,128)(2,1)} %collective-permute-done.6.a_up, ...), custom_call_target="tpu_custom_call" | custom-call | flops 275000000 | bytes 750000 | tf_op jit(solution)/shard_map/attend_step/pallas_call | solution.py:514
  59.6 5.5 %collective-permute-done.5.got_ref = bf16[80,256]{1,0:T(8,128)(2,1)S(1)} collective-permute-done((bf16[80,256]{1,0:T(8,128)(2,1)S(1)}, bf16[80,256]{1,0:T(8,128)(2,1)S(1)}, u32[]{:S(2)}, u32[]{:S(2)}) %collective-permute-start.5) | collective-permute-done | bytes 40992 | tf_op jit(solution)/shard_map/ppermute | solution.py:479
  65.1 0.6 grow.4
  65.8 3.7 %collective-permute-start.18 = (bf16[2,2,128,384]{3,2,1,0:T(8,128)(2,1)S(1)}, bf16[2,2,128,384]{3,2,1,0:T(8,128)(2,1)S(1)}, u32[]{:S(2)}, u32[]{:S(2)}) collective-permute-start(bf16[2,2,128,384]{3,2,1,0:T(8,128)(2,1)S(1)} %collective-permute-done.13.b_up), channel_id=1, source_target_pairs={{0,112},{8,120},{16,0},{24,8},{32,16},{40,24},{48,32},{56,40},{64,... | collective-permute-start | bytes 1179656 | tf_op jit(solution)/shard_map/ppermute | solution.py:475
  69.5 3.4 %collective-permute-start.10 = (bf16[80,256]{1,0:T(8,128)(2,1)S(1)}, bf16[80,256]{1,0:T(8,128)(2,1)S(1)}, u32[]{:S(2)}, u32[]{:S(2)}) collective-permute-start(bf16[80,256]{1,0:T(8,128)(2,1)S(1)} %get-tuple-element.124), channel_id=1, source_target_pairs={{0,64},{8,72},{16,80},{24,88},{32,96},{40,104},{48,112},{56,120},{... | collective-permute-start | bytes 122888 | tf_op jit(solution)/shard_map/ppermute | solution.py:479
  72.9 4.4 %scan_inside.3.z_ref = f32[2,1024,128]{2,1,0:T(8,128)S(1)} custom-call(s32[4]{0:T(128)S(1)} %copy-done.5, s32[32]{0:T(128)S(1)} %copy-done.6, bf16[8,128,384]{2,1,0:T(8,128)(2,1)S(1)} %all-to-all-done.in_ref), custom_call_target="tpu_custom_call" | custom-call | flops 440000000 | bytes 1200000 | tf_op jit(solution)/shard_map/scan_inside/pallas_call | solution.py:568
  77.3 2.7 %attend_step.4 = (f32[2,8,256]{2,1,0:T(8,128)S(1)}, f32[2,8,256]{2,1,0:T(8,128)S(1)}, f32[2,3,128,256]{3,2,1,0:T(8,128)S(1)}) custom-call(s32[4]{0:T(128)S(1)} %copy-done.5, s32[32,32]{1,0:T(8,128)S(1)} %copy-done.4, bf16[2,2,128,384]{3,2,1,0:T(8,128)(2,1)S(1)} %get-tuple-element.106.q_ref, bf16[2,2,128,384]{3,2,1,0:T(8,128)(2,1)} %collective-permute-done.11.a_up, ...), custom_call_target="tpu_custom_call" | custom-call | flops 275000000 | bytes 750000 | tf_op jit(solution)/shard_map/attend_step/pallas_call | solution.py:514
  80.0 1.2 %grow.5 = (f32[72,256]{1,0:T(8,128)S(1)}, f32[72,256]{1,0:T(8,128)}, bf16[80,256]{1,0:T(8,128)(2,1)S(1)}) custom-call(s32[4]{0:T(128)S(1)} %copy-done.5, bf16[80,256]{1,0:T(8,128)(2,1)S(1)} %collective-permute-done.10.got_ref, f32[72,256]{1,0:T(8,128)S(1)} %get-tuple-element.144.total_in, f32[72,256]{1,0:T(8,128)S(1)} %get-tuple-element.145.rest_0_), custom_call_target="tpu_custom_call" | custom-call | flops 55000000 | bytes 150000 | tf_op jit(solution)/shard_map/grow/pallas_call | solution.py:579
  81.3 1.3 %collective-permute-start.22 = (bf16[2,2,128,384]{3,2,1,0:T(8,128)(2,1)}, bf16[2,2,128,384]{3,2,1,0:T(8,128)(2,1)}, u32[]{:S(2)}, u32[]{:S(2)}) collective-permute-start(bf16[2,2,128,384]{3,2,1,0:T(8,128)(2,1)} %collective-permute-done.19.b_down), channel_id=1, source_target_pairs={{0,16},{8,24},{16,32},{24,40},{32,48},{40,56},{48,64},{56,72},{64,... | collective-permute-start | bytes 1179656 | tf_op jit(solution)/shard_map/ppermute | solution.py:475
  82.7 3.2 %collective-permute-start.17 = (bf16[80,256]{1,0:T(8,128)(2,1)S(1)}, bf16[80,256]{1,0:T(8,128)(2,1)S(1)}, u32[]{:S(2)}, u32[]{:S(2)}) collective-permute-start(bf16[80,256]{1,0:T(8,128)(2,1)S(1)} %get-tuple-element.146), channel_id=1, source_target_pairs={{0,128},{8,136},{16,144},{24,152},{32,160},{40,168},{48,176},{56,1... | collective-permute-start | bytes 122888 | tf_op jit(solution)/shard_map/ppermute | solution.py:479
  85.8 2.7 %attend_step.5 = (f32[2,8,256]{2,1,0:T(8,128)S(1)}, f32[2,8,256]{2,1,0:T(8,128)S(1)}, f32[2,3,128,256]{3,2,1,0:T(8,128)S(1)}) custom-call(s32[4]{0:T(128)S(1)} %copy-done.5, s32[32,32]{1,0:T(8,128)S(1)} %copy-done.4, bf16[2,2,128,384]{3,2,1,0:T(8,128)(2,1)S(1)} %get-tuple-element.106.q_ref, bf16[2,2,128,384]{3,2,1,0:T(8,128)(2,1)} %collective-permute-done.15.a_up, ...), custom_call_target="tpu_custom_call" | custom-call | flops 275000000 | bytes 750000 | tf_op jit(solution)/shard_map/attend_step/pallas_call | solution.py:514
  88.5 0.9 copy-done
  90.0 4.1 %collective-permute-start.20 = (bf16[64,256]{1,0:T(8,128)(2,1)S(1)}, bf16[64,256]{1,0:T(8,128)(2,1)S(1)}, u32[]{:S(2)}, u32[]{:S(2)}) collective-permute-start(bf16[64,256]{1,0:T(8,128)(2,1)S(1)} %last_before.1.before_ref), channel_id=1, source_target_pairs={{0,8},{8,0},{16,24},{24,16},{32,40},{40,32},{48,56},{56,48},{64,72... | collective-permute-start | bytes 98312 | tf_op jit(solution)/shard_map/ppermute | solution.py:479
  94.1 0.8 dynamic_slice.3
  95.0 2.4 %scan_finish.1 = bf16[8,192,128]{2,1,0:T(8,128)(2,1)S(1)} custom-call(s32[4]{0:T(128)S(1)} %copy-done.5, bf16[8,128,384]{2,1,0:T(8,128)(2,1)S(1)} %all-to-all-done.in_ref, f32[2,1024,128]{2,1,0:T(8,128)S(1)} %scan_inside.2.y_ref, f32[2,1024,128]{2,1,0:T(8,128)S(1)} %scan_inside.3.z_ref, f32[8,8,128]{2,1,0:T(8,128)S(1)} %get-tuple-element.141.row_ref, ...), custom_call_target="tpu_custom_call" | custom-call | flops 330000000 | bytes 900000 | tf_op jit(solution)/shard_map/scan_finish/pallas_call | solution.py:594
  97.4 0.7 copy-done.2
  98.1 5.0 %all-to-all-start.1 = ((bf16[8,192,128]{2,1,0:T(8,128)(2,1)}), bf16[8,192,128]{2,1,0:T(8,128)(2,1)S(1)}, u32[]{:S(2)}, u32[]{:S(2)}) async-start(bf16[8,192,128]{2,1,0:T(8,128)(2,1)} %copy-done.2), calls=%async_computation.1 | async-start | bytes 786432 | tf_op jit(solution)/shard_map/all_to_all | solution.py:606
  103.1 2.1 %attend_last.2 = (bf16[128,384]{1,0:T(8,128)(2,1)S(1)}, bf16[128,384]{1,0:T(8,128)(2,1)S(1)}) custom-call(s32[4]{0:T(128)S(1)} %copy-done.5, s32[32,32]{1,0:T(8,128)S(1)} %copy-done.4, bf16[2,2,128,384]{3,2,1,0:T(8,128)(2,1)S(1)} %get-tuple-element.106.q_ref, bf16[2,2,128,384]{3,2,1,0:T(8,128)(2,1)} %collective-permute-done.21.a_ref, ...), custom_call_target="tpu_custom_call" | custom-call | flops 220000000 | bytes 600000 | tf_op jit(solution)/shard_map/attend_last/pallas_call | solution.py:611
  105.2 2.1 %attend_last.3 = (bf16[128,384]{1,0:T(8,128)(2,1)S(1)}, bf16[128,384]{1,0:T(8,128)(2,1)S(1)}) custom-call(s32[4]{0:T(128)S(1)} %copy-done.5, s32[32,32]{1,0:T(8,128)S(1)} %copy-done.4, bf16[2,2,128,384]{3,2,1,0:T(8,128)(2,1)S(1)} %get-tuple-element.106.q_ref, bf16[2,2,128,384]{3,2,1,0:T(8,128)(2,1)} %collective-permute-done.21.a_ref, ...), custom_call_target="tpu_custom_call" | custom-call | flops 220000000 | bytes 600000 | tf_op jit(solution)/shard_map/attend_last/pallas_call | solution.py:611
  107.4 0.7 collective-permute-start.23
  108.1 2.1 %collective-permute-start.24 = (bf16[128,384]{1,0:T(8,128)(2,1)S(1)}, bf16[128,384]{1,0:T(8,128)(2,1)S(1)}, u32[]{:S(2)}, u32[]{:S(2)}) collective-permute-start(bf16[128,384]{1,0:T(8,128)(2,1)S(1)} %get-tuple-element.175), channel_id=1, source_target_pairs={{0,128},{8,136},{16,144},{24,152},{32,160},{40,168},{48,176},{56,1... | collective-permute-start | bytes 294920 | tf_op jit(solution)/shard_map/ppermute | solution.py:479
  110.2 1.1 collective-permute-start.25
  111.3 2.6 %collective-permute-done.24.rest_2_ = bf16[128,384]{1,0:T(8,128)(2,1)S(1)} collective-permute-done((bf16[128,384]{1,0:T(8,128)(2,1)S(1)}, bf16[128,384]{1,0:T(8,128)(2,1)S(1)}, u32[]{:S(2)}, u32[]{:S(2)}) %collective-permute-start.24) | collective-permute-done | bytes 98336 | tf_op jit(solution)/shard_map/ppermute | solution.py:479
  114.0 2.5 %collective-permute-done.25.rest_3_ = bf16[128,384]{1,0:T(8,128)(2,1)S(1)} collective-permute-done((bf16[128,384]{1,0:T(8,128)(2,1)S(1)}, bf16[128,384]{1,0:T(8,128)(2,1)S(1)}, u32[]{:S(2)}, u32[]{:S(2)}) %collective-permute-start.25) | collective-permute-done | bytes 98336 | tf_op jit(solution)/shard_map/ppermute | solution.py:479
  116.5 1.5 %add_up.1 = bf16[128,1536]{1,0:T(8,128)(2,1)} custom-call(s32[4]{0:T(128)S(1)} %copy-done.5, bf16[8,192,128]{2,1,0:T(8,128)(2,1)S(1)} %all-to-all-done.1.scan_ref, bf16[128,384]{1,0:T(8,128)(2,1)S(1)} %get-tuple-element.173.rest_0_, bf16[128,384]{1,0:T(8,128)(2,1)S(1)} %collective-permute-done.23.rest_1_, ...), custom_call_target="tpu_custom_call" | custom-call | flops 165000000 | bytes 450000 | tf_op jit(solution)/shard_map/add_up/pallas_call | solution.py:621
  (48 shorter events, 2.4 us)
Async XLA Ops:
  2.9 7.3 %collective-permute-start = (bf16[3,128,384]{2,1,0:T(8,128)(2,1)}, bf16[3,128,384]{2,1,0:T(8,128)(2,1)S(1)}, u32[]{:S(2)}, u32[]{:S(2)}) collective-permute-start(bf16[3,128,384]{2,1,0:T(8,128)(2,1)} %get-tuple-element.92), channel_id=1, source_target_pairs={{0,8},{8,0},{16,24},{24,16},{32,40},{40,32},{48,56},{56,48},{64,72... | collective-permute-start | bytes 884744 | tf_op jit(solution)/shard_map/ppermute | solution.py:479
  6.2 16.8 %collective-permute-start.3 = (bf16[3,128,384]{2,1,0:T(8,128)(2,1)}, bf16[3,128,384]{2,1,0:T(8,128)(2,1)S(1)}, u32[]{:S(2)}, u32[]{:S(2)}) collective-permute-start(bf16[3,128,384]{2,1,0:T(8,128)(2,1)} %get-tuple-element.98), channel_id=1, source_target_pairs={{0,128},{8,136},{16,144},{24,152},{32,160},{40,168},{48,176},{56,1... | collective-permute-start | bytes 884744 | tf_op jit(solution)/shard_map/ppermute | solution.py:479
  7.2 15.8 %collective-permute-start.4 = (bf16[3,128,384]{2,1,0:T(8,128)(2,1)}, bf16[3,128,384]{2,1,0:T(8,128)(2,1)S(1)}, u32[]{:S(2)}, u32[]{:S(2)}) collective-permute-start(bf16[3,128,384]{2,1,0:T(8,128)(2,1)} %get-tuple-element.99), channel_id=1, source_target_pairs={{0,136},{8,128},{16,152},{24,144},{32,168},{40,160},{48,184},{56,1... | collective-permute-start | bytes 884744 | tf_op jit(solution)/shard_map/ppermute | solution.py:479
  10.4 16.6 %collective-permute-start.6 = (bf16[2,2,128,384]{3,2,1,0:T(8,128)(2,1)S(1)}, bf16[2,2,128,384]{3,2,1,0:T(8,128)(2,1)}, u32[]{:S(2)}, u32[]{:S(2)}) collective-permute-start(bf16[2,2,128,384]{3,2,1,0:T(8,128)(2,1)S(1)} %pad_maximum_fusion), channel_id=1, source_target_pairs={{0,112},{8,120},{16,0},{24,8},{32,16},{40,24},{48,32},{56,40},{64,... | collective-permute-start | bytes 1179656 | tf_op jit(solution)/shard_map/ppermute | solution.py:475
  14.3 15.4 %collective-permute-start.7 = (bf16[2,2,128,384]{3,2,1,0:T(8,128)(2,1)S(1)}, bf16[2,2,128,384]{3,2,1,0:T(8,128)(2,1)}, u32[]{:S(2)}, u32[]{:S(2)}) collective-permute-start(bf16[2,2,128,384]{3,2,1,0:T(8,128)(2,1)S(1)} %pad_maximum_fusion), channel_id=1, source_target_pairs={{0,16},{8,24},{16,32},{24,40},{32,48},{40,56},{48,64},{56,72},{64,... | collective-permute-start | bytes 1179656 | tf_op jit(solution)/shard_map/ppermute | solution.py:475
  16.3 22.1 %all-to-all-start = ((bf16[8,128,384]{2,1,0:T(8,128)(2,1)}), bf16[8,128,384]{2,1,0:T(8,128)(2,1)S(1)}, u32[]{:S(2)}, u32[]{:S(2)}) async-start(bf16[8,128,384]{2,1,0:T(8,128)(2,1)} %scan_pack.1), calls=%async_computation | async-start | bytes 1572864 | tf_op jit(solution)/shard_map/all_to_all | solution.py:500
  23.0 15.4 %copy-start.5 = (s32[4]{0:T(128)S(1)}, s32[4]{0:T(128)}, u32[]{:S(2)}) copy-start(s32[4]{0:T(128)} %pad_add_fusion.ids) | copy-start | bytes 52
  23.0 15.4 %copy-start.6 = (s32[32]{0:T(128)S(1)}, s32[32]{0:T(128)}, u32[]{:S(2)}) copy-start(s32[32]{0:T(128)} %order_ref.5) | copy-start | bytes 388
  23.1 12.1 %collective-permute-start.8 = (bf16[2,2,128,384]{3,2,1,0:T(8,128)(2,1)S(1)}, bf16[2,2,128,384]{3,2,1,0:T(8,128)(2,1)}, u32[]{:S(2)}, u32[]{:S(2)}) collective-permute-start(bf16[2,2,128,384]{3,2,1,0:T(8,128)(2,1)S(1)} %pad_maximum_fusion.1), channel_id=1, source_target_pairs={{0,112},{8,120},{16,0},{24,8},{32,16},{40,24},{48,32},{56,40},{64,... | collective-permute-start | bytes 1179656 | tf_op jit(solution)/shard_map/ppermute | solution.py:475
  27.0 11.4 %collective-permute-start.9 = (bf16[2,2,128,384]{3,2,1,0:T(8,128)(2,1)S(1)}, bf16[2,2,128,384]{3,2,1,0:T(8,128)(2,1)}, u32[]{:S(2)}, u32[]{:S(2)}) collective-permute-start(bf16[2,2,128,384]{3,2,1,0:T(8,128)(2,1)S(1)} %pad_maximum_fusion.1), channel_id=1, source_target_pairs={{0,16},{8,24},{16,32},{24,40},{32,48},{40,56},{48,64},{56,72},{64,... | collective-permute-start | bytes 1179656 | tf_op jit(solution)/shard_map/ppermute | solution.py:475
  27.0 25.7 %collective-permute-start.11 = (bf16[2,2,128,384]{3,2,1,0:T(8,128)(2,1)}, bf16[2,2,128,384]{3,2,1,0:T(8,128)(2,1)}, u32[]{:S(2)}, u32[]{:S(2)}) collective-permute-start(bf16[2,2,128,384]{3,2,1,0:T(8,128)(2,1)} %collective-permute-done.6.a_up), channel_id=1, source_target_pairs={{0,112},{8,120},{16,0},{24,8},{32,16},{40,24},{48,32},{56,40},{64,... | collective-permute-start | bytes 1179656 | tf_op jit(solution)/shard_map/ppermute | solution.py:475
  29.7 23.0 %collective-permute-start.12 = (bf16[2,2,128,384]{3,2,1,0:T(8,128)(2,1)}, bf16[2,2,128,384]{3,2,1,0:T(8,128)(2,1)}, u32[]{:S(2)}, u32[]{:S(2)}) collective-permute-start(bf16[2,2,128,384]{3,2,1,0:T(8,128)(2,1)} %collective-permute-done.7.a_down), channel_id=1, source_target_pairs={{0,16},{8,24},{16,32},{24,40},{32,48},{40,56},{48,64},{56,72},{64,... | collective-permute-start | bytes 1179656 | tf_op jit(solution)/shard_map/ppermute | solution.py:475
  40.6 25.1 %collective-permute-start.13 = (bf16[2,2,128,384]{3,2,1,0:T(8,128)(2,1)}, bf16[2,2,128,384]{3,2,1,0:T(8,128)(2,1)S(1)}, u32[]{:S(2)}, u32[]{:S(2)}) collective-permute-start(bf16[2,2,128,384]{3,2,1,0:T(8,128)(2,1)} %collective-permute-done.8.b_up), channel_id=1, source_target_pairs={{0,112},{8,120},{16,0},{24,8},{32,16},{40,24},{48,32},{56,40},{64,... | collective-permute-start | bytes 1179656 | tf_op jit(solution)/shard_map/ppermute | solution.py:475
  41.0 24.7 %collective-permute-start.14 = (bf16[2,2,128,384]{3,2,1,0:T(8,128)(2,1)}, bf16[2,2,128,384]{3,2,1,0:T(8,128)(2,1)S(1)}, u32[]{:S(2)}, u32[]{:S(2)}) collective-permute-start(bf16[2,2,128,384]{3,2,1,0:T(8,128)(2,1)} %collective-permute-done.9.b_down), channel_id=1, source_target_pairs={{0,16},{8,24},{16,32},{24,40},{32,48},{40,56},{48,64},{56,72},{64,... | collective-permute-start | bytes 1179656 | tf_op jit(solution)/shard_map/ppermute | solution.py:475
  42.2 6.3 %copy-start.3 = (bf16[3,128,384]{2,1,0:T(8,128)(2,1)S(1)}, bf16[3,128,384]{2,1,0:T(8,128)(2,1)}, u32[]{:S(2)}) copy-start(bf16[3,128,384]{2,1,0:T(8,128)(2,1)} %get-tuple-element.97.own) | copy-start | bytes 884740
  43.6 4.1 %collective-permute-start.1 = (bf16[2,80,256]{2,1,0:T(8,128)(2,1)S(1)}, bf16[2,80,256]{2,1,0:T(8,128)(2,1)S(1)}, u32[]{:S(2)}, u32[]{:S(2)}) collective-permute-start(bf16[2,80,256]{2,1,0:T(8,128)(2,1)S(1)} %get-tuple-element.95), channel_id=1, source_target_pairs={{0,8},{8,0},{16,24},{24,16},{32,40},{40,32},{48,56},{56,48},{64,72... | collective-permute-start | bytes 245768 | tf_op jit(solution)/shard_map/ppermute | solution.py:479
  47.6 0.9 copy-start.4
  48.2 3.9 %collective-permute-start.2 = (bf16[80,256]{1,0:T(8,128)(2,1)S(1)}, bf16[80,256]{1,0:T(8,128)(2,1)S(1)}, u32[]{:S(2)}, u32[]{:S(2)}) collective-permute-start(bf16[80,256]{1,0:T(8,128)(2,1)S(1)} %get-tuple-element.96), channel_id=1, source_target_pairs={{0,16},{8,24},{16,0},{24,8},{32,48},{40,56},{48,32},{56,40},{64,80... | collective-permute-start | bytes 122888 | tf_op jit(solution)/shard_map/ppermute | solution.py:479
  52.7 20.2 %collective-permute-start.15 = (bf16[2,2,128,384]{3,2,1,0:T(8,128)(2,1)}, bf16[2,2,128,384]{3,2,1,0:T(8,128)(2,1)}, u32[]{:S(2)}, u32[]{:S(2)}) collective-permute-start(bf16[2,2,128,384]{3,2,1,0:T(8,128)(2,1)} %collective-permute-done.11.a_up), channel_id=1, source_target_pairs={{0,112},{8,120},{16,0},{24,8},{32,16},{40,24},{48,32},{56,40},{64,... | collective-permute-start | bytes 1179656 | tf_op jit(solution)/shard_map/ppermute | solution.py:475
  56.8 16.1 %collective-permute-start.16 = (bf16[2,2,128,384]{3,2,1,0:T(8,128)(2,1)}, bf16[2,2,128,384]{3,2,1,0:T(8,128)(2,1)S(1)}, u32[]{:S(2)}, u32[]{:S(2)}) collective-permute-start(bf16[2,2,128,384]{3,2,1,0:T(8,128)(2,1)} %collective-permute-done.12.a_down), channel_id=1, source_target_pairs={{0,16},{8,24},{16,32},{24,40},{32,48},{40,56},{48,64},{56,72},{64,... | collective-permute-start | bytes 1179656 | tf_op jit(solution)/shard_map/ppermute | solution.py:475
  56.8 8.3 %collective-permute-start.5 = (bf16[80,256]{1,0:T(8,128)(2,1)S(1)}, bf16[80,256]{1,0:T(8,128)(2,1)S(1)}, u32[]{:S(2)}, u32[]{:S(2)}) collective-permute-start(bf16[80,256]{1,0:T(8,128)(2,1)S(1)} %get-tuple-element.105), channel_id=1, source_target_pairs={{0,32},{8,40},{16,48},{24,56},{32,0},{40,8},{48,16},{56,24},{64,96... | collective-permute-start | bytes 122888 | tf_op jit(solution)/shard_map/ppermute | solution.py:479
  65.7 15.5 %collective-permute-start.19 = (bf16[2,2,128,384]{3,2,1,0:T(8,128)(2,1)S(1)}, bf16[2,2,128,384]{3,2,1,0:T(8,128)(2,1)}, u32[]{:S(2)}, u32[]{:S(2)}) collective-permute-start(bf16[2,2,128,384]{3,2,1,0:T(8,128)(2,1)S(1)} %collective-permute-done.14.b_down), channel_id=1, source_target_pairs={{0,16},{8,24},{16,32},{24,40},{32,48},{40,56},{48,64},{56,72},{64,... | collective-permute-start | bytes 1179656 | tf_op jit(solution)/shard_map/ppermute | solution.py:475
  65.8 20.0 %collective-permute-start.18 = (bf16[2,2,128,384]{3,2,1,0:T(8,128)(2,1)S(1)}, bf16[2,2,128,384]{3,2,1,0:T(8,128)(2,1)S(1)}, u32[]{:S(2)}, u32[]{:S(2)}) collective-permute-start(bf16[2,2,128,384]{3,2,1,0:T(8,128)(2,1)S(1)} %collective-permute-done.13.b_up), channel_id=1, source_target_pairs={{0,112},{8,120},{16,0},{24,8},{32,16},{40,24},{48,32},{56,40},{64,... | collective-permute-start | bytes 1179656 | tf_op jit(solution)/shard_map/ppermute | solution.py:475
  69.5 10.5 %collective-permute-start.10 = (bf16[80,256]{1,0:T(8,128)(2,1)S(1)}, bf16[80,256]{1,0:T(8,128)(2,1)S(1)}, u32[]{:S(2)}, u32[]{:S(2)}) collective-permute-start(bf16[80,256]{1,0:T(8,128)(2,1)S(1)} %get-tuple-element.124), channel_id=1, source_target_pairs={{0,64},{8,72},{16,80},{24,88},{32,96},{40,104},{48,112},{56,120},{... | collective-permute-start | bytes 122888 | tf_op jit(solution)/shard_map/ppermute | solution.py:479
  81.2 21.9 %collective-permute-start.21 = (bf16[2,2,128,384]{3,2,1,0:T(8,128)(2,1)}, bf16[2,2,128,384]{3,2,1,0:T(8,128)(2,1)}, u32[]{:S(2)}, u32[]{:S(2)}) collective-permute-start(bf16[2,2,128,384]{3,2,1,0:T(8,128)(2,1)} %collective-permute-done.15.a_up), channel_id=1, source_target_pairs={{0,112},{8,120},{16,0},{24,8},{32,16},{40,24},{48,32},{56,40},{64,... | collective-permute-start | bytes 1179656 | tf_op jit(solution)/shard_map/ppermute | solution.py:475
  81.3 21.8 %collective-permute-start.22 = (bf16[2,2,128,384]{3,2,1,0:T(8,128)(2,1)}, bf16[2,2,128,384]{3,2,1,0:T(8,128)(2,1)}, u32[]{:S(2)}, u32[]{:S(2)}) collective-permute-start(bf16[2,2,128,384]{3,2,1,0:T(8,128)(2,1)} %collective-permute-done.19.b_down), channel_id=1, source_target_pairs={{0,16},{8,24},{16,32},{24,40},{32,48},{40,56},{48,64},{56,72},{64,... | collective-permute-start | bytes 1179656 | tf_op jit(solution)/shard_map/ppermute | solution.py:475
  82.7 6.8 %collective-permute-start.17 = (bf16[80,256]{1,0:T(8,128)(2,1)S(1)}, bf16[80,256]{1,0:T(8,128)(2,1)S(1)}, u32[]{:S(2)}, u32[]{:S(2)}) collective-permute-start(bf16[80,256]{1,0:T(8,128)(2,1)S(1)} %get-tuple-element.146), channel_id=1, source_target_pairs={{0,128},{8,136},{16,144},{24,152},{32,160},{40,168},{48,176},{56,1... | collective-permute-start | bytes 122888 | tf_op jit(solution)/shard_map/ppermute | solution.py:479
  88.5 0.9 copy-start
  90.0 5.0 %collective-permute-start.20 = (bf16[64,256]{1,0:T(8,128)(2,1)S(1)}, bf16[64,256]{1,0:T(8,128)(2,1)S(1)}, u32[]{:S(2)}, u32[]{:S(2)}) collective-permute-start(bf16[64,256]{1,0:T(8,128)(2,1)S(1)} %last_before.1.before_ref), channel_id=1, source_target_pairs={{0,8},{8,0},{16,24},{24,16},{32,40},{40,32},{48,56},{56,48},{64,72... | collective-permute-start | bytes 98312 | tf_op jit(solution)/shard_map/ppermute | solution.py:479
  97.4 0.7 copy-start.2
  98.1 5.0 %copy-start.1 = (f32[2,3,128,256]{3,2,1,0:T(8,128)S(1)}, f32[2,3,128,256]{3,2,1,0:T(8,128)}, u32[]{:S(2)}) copy-start(f32[2,3,128,256]{3,2,1,0:T(8,128)} %copy-done) | copy-start | bytes 2359300
  98.1 13.2 %all-to-all-start.1 = ((bf16[8,192,128]{2,1,0:T(8,128)(2,1)}), bf16[8,192,128]{2,1,0:T(8,128)(2,1)S(1)}, u32[]{:S(2)}, u32[]{:S(2)}) async-start(bf16[8,192,128]{2,1,0:T(8,128)(2,1)} %copy-done.2), calls=%async_computation.1 | async-start | bytes 786432 | tf_op jit(solution)/shard_map/all_to_all | solution.py:606
  107.4 4.0 %collective-permute-start.23 = (bf16[128,384]{1,0:T(8,128)(2,1)S(1)}, bf16[128,384]{1,0:T(8,128)(2,1)S(1)}, u32[]{:S(2)}, u32[]{:S(2)}) collective-permute-start(bf16[128,384]{1,0:T(8,128)(2,1)S(1)} %get-tuple-element.174), channel_id=1, source_target_pairs={{0,8},{8,0},{16,24},{24,16},{32,40},{40,32},{48,56},{56,48},{64,72... | collective-permute-start | bytes 294920 | tf_op jit(solution)/shard_map/ppermute | solution.py:479
  108.1 5.9 %collective-permute-start.24 = (bf16[128,384]{1,0:T(8,128)(2,1)S(1)}, bf16[128,384]{1,0:T(8,128)(2,1)S(1)}, u32[]{:S(2)}, u32[]{:S(2)}) collective-permute-start(bf16[128,384]{1,0:T(8,128)(2,1)S(1)} %get-tuple-element.175), channel_id=1, source_target_pairs={{0,128},{8,136},{16,144},{24,152},{32,160},{40,168},{48,176},{56,1... | collective-permute-start | bytes 294920 | tf_op jit(solution)/shard_map/ppermute | solution.py:479
  110.2 6.3 %collective-permute-start.25 = (bf16[128,384]{1,0:T(8,128)(2,1)S(1)}, bf16[128,384]{1,0:T(8,128)(2,1)S(1)}, u32[]{:S(2)}, u32[]{:S(2)}) collective-permute-start(bf16[128,384]{1,0:T(8,128)(2,1)S(1)} %get-tuple-element.176), channel_id=1, source_target_pairs={{0,136},{8,128},{16,152},{24,144},{32,168},{40,160},{48,184},{56,1... | collective-permute-start | bytes 294920 | tf_op jit(solution)/shard_map/ppermute | solution.py:479
where the time goes:
time: 118 us
  starting transfers between devices  55.9 us (47%)
  Pallas kernels  33.7 us (29%)
  waiting for transfers between devices  24 us (20%)
  local copies, waits for them, and re-layouts  3.44 us (3%)
    ppermute x12, starting transfers between devices, partner(): return lax.ppermute(array, 'tm', [(i, i ^ bits) for i in range(N_TM)])  24.4 us
    ppermute x14, starting transfers between devices, z_shift(): return lax.ppermute(array, 'tm', pairs)  21.4 us
    ppermute x12, waiting for transfers between devices, partner(): return lax.ppermute(array, 'tm', [(i, i ^ bits) for i in range(N_TM)])  15.2 us
    ppermute x14, waiting for transfers between devices, z_shift(): return lax.ppermute(array, 'tm', pairs)  8.75 us
    pallas_call x3, Pallas kernels, step_of(): call(functools.partial(attend_step, step), STATE, 2, 8, 2.5)  8.13 us
    all_to_all x1, starting transfers between devices, on_device(): lax.all_to_all(sent, 'space', split_axis=0, concat_axis=0, tiled=True)  5.12 us
    all_to_all x1, starting transfers between devices, on_device(): lax.all_to_all(normed, 'space', split_axis=0, concat_axis=0, tiled=True)  4.96 us
    pallas_call x1, Pallas kernels, on_device(): call(functools.partial(scan_inside, True), wide, 2, 1, 4, [pltpu.VMEM((2,...  4.38 us
  transfers between devices with their start and end apart: 28, of which 9 were waited for; matrix products, arithmetic and copies ran while one was open for 2% of the time, Pallas kernels for 25%

commit v1 on v0

--- a/solution.py
+++ b/solution.py
@@ -21,7 +21,7 @@
 WIN = 256
 ROWS = STATE_DIM + 8
 
-COST = 0.1
+COST = 0.001
 EPS = 1e-05
 FLOOR = -1e30
 LOG2_SCALE = HEAD_DIM ** (-0.5) * math.log2(math.e)
@@ -492,13 +492,13 @@
     from_core = partner(to_core, 1)
     from_half = partner(to_half, 16)
     from_both = partner(to_both, 17)
-    chunks = {(0, 0): jnp.stack([own[1:], from_core[1:]])}
-    inner_x, _ = tie(inner_x, chunks[0, 0])
+    inner_x, _ = tie(inner_x, from_core)
     sent = call(
         scan_pack, jax.ShapeDtypeStruct((N_SPACE, TOKENS, WIN + 128), BF16), 0, 3, 1.5, vmem=56
     )(inner_x, bc_proj, log_decay)
     frame_in = lax.all_to_all(sent, "space", split_axis=0, concat_axis=0, tiled=True)
-
+    (own, from_core), _ = tie((own, from_core), sent)
+    chunks = {(0, 0): jnp.stack([own[1:], from_core[1:]])}
 
     def pass_on(source, step, after=None):
         if after is not None:
@@ -537,34 +537,32 @@
     total, walk = call(chip_state, (one, sent), 1, 2, 0.5)(ids, state, core_sent)
 
     other = partner(walk, 2)
+    frame_tokens = N_SPACE * TOKENS
+    wide = jax.ShapeDtypeStruct((2, frame_tokens, 128), F32)
+    inside_in, _ = tie(frame_in, walk)
+    y_row = call(
+        functools.partial(scan_inside, False), wide, 2, 1, 2, [pltpu.VMEM((8, 128), F32)]
+    )(ids, col_order, inside_in)
+    pass_on(0, 3, y_row)
+    other, y_row = tie(other, y_row)
+    before, total, walk = call(functools.partial(grow, 2), (one, one, sent), 1, 2, 0.5)(
+        ids, other, total
+    )
+
+    other = partner(walk, 4)
     own, _ = tie(own, walk)
     *flash, q_all = call(
         attend_own, STATE + (jax.ShapeDtypeStruct((2, 2, TOKENS, GROUP), BF16),), 2, 4, 2
     )(ids, tile_mask, own, from_core, from_half, from_both)
+    pass_on(1, 2, flash)
+    flash = step_of(1, flash)
     other, flash = tie(other, flash)
-    before, total, walk = call(functools.partial(grow, 2), (one, one, sent), 1, 2, 0.5)(
-        ids, other, total
-    )
-
-    other = partner(walk, 4)
-    frame_tokens = N_SPACE * TOKENS
-    wide = jax.ShapeDtypeStruct((2, frame_tokens, 128), F32)
-    pass_on(0, 3, walk)
-    inside_in, _ = tie(frame_in, pair(1, 1))
-    y_row = call(
-        functools.partial(scan_inside, False), wide, 2, 1, 2, [pltpu.VMEM((8, 128), F32)]
-    )(ids, col_order, inside_in)
-    pass_on(1, 2, y_row)
-    flash, y_row = tie(flash, y_row)
-    flash = step_of(1, flash)
-    other, flash, y_row = tie(other, flash, y_row)
     before, total, walk = call(functools.partial(grow, 4), (one, one, sent), 1, 3, 0.5)(
         ids, other, total, before
     )
 
-    other = partner(walk, 8)
-    pass_on(1, 3, walk)
-    inside_in, _, _ = tie(inside_in, walk, pair(0, 3))
+    other = partner(walk, 14)
+    inside_in, _ = tie(frame_in, walk)
     y_col = call(
         functools.partial(scan_inside, True),
         wide,
@@ -573,22 +571,22 @@
         4,
         [pltpu.VMEM((2, 3, frame_tokens, 128), F32)],
     )(ids, col_order, inside_in)
-    flash, y_col = tie(flash, y_col)
-    flash = step_of(2, flash)
-    other, flash, y_col = tie(other, flash, y_col)
+    other, y_col = tie(other, y_col)
     before, total, walk = call(functools.partial(grow, 8), (one, one, sent), 1, 3, 0.5)(
         ids, other, total, before
     )
 
     other = partner(walk, 16)
-    (to_up, to_down), flash, walk = tie((chunks[0, 3], chunks[1, -3]), flash, walk)
-    far_a, far_b = z_shift(to_up, -1), z_shift(to_down, 1)
-    flash = step_of(3, flash)
+    pass_on(1, 3, walk)
+    flash, _ = tie(flash, walk)
+    flash = step_of(2, flash)
     other, flash = tie(other, flash)
     before = call(last_before, jax.ShapeDtypeStruct((STATE_DIM, WIN), BF16), 1, 2, 0.5)(
         ids, other, before
     )
     before_other = partner(before, 1)
+    (to_up, to_down), _ = tie((chunks[0, 3], chunks[1, -3]), before)
+    far_a, far_b = z_shift(to_up, -1), z_shift(to_down, 1)
 
     gain = lax.dynamic_slice(norm_gain, (384 * (tile // 2) + 128 * (tile % 2),), (WIN,))
     normed = call(scan_finish, jax.ShapeDtypeStruct((N_SPACE, 192, 128), BF16), 1, 9, 3)(
@@ -605,6 +603,7 @@
     )
     scan_rows = lax.all_to_all(normed, "space", split_axis=0, concat_axis=0, tiled=True)
     flash, _ = tie(flash, normed)
+    flash = step_of(3, flash)
     piece = jax.ShapeDtypeStruct((TOKENS, GROUP), BF16)
     pieces = {}
     for u in (1, 0):

time: 118 us -> 114 us (0.966)
  waiting for transfers between devices: 24 us -> 20.3 us
    ppermute x14, waiting for transfers between devices: 8.75 us -> 0.04 us  [z_shift(): return lax.ppermute(array, 'tm', pairs)]
    all_to_all x1, waiting for transfers between devices: 0.01 us -> 4.02 us  [on_device(): lax.all_to_all(sent, 'space', split_axis=0, concat_axis=0, tiled=True)]
    all_to_all x1, starting transfers between devices: 5.12 us -> 3.68 us  [on_device(): lax.all_to_all(sent, 'space', split_axis=0, concat_axis=0, tiled=True)]
    all_to_all x1, starting transfers between devices: 4.96 us -> 3.58 us  [on_device(): lax.all_to_all(normed, 'space', split_axis=0, concat_axis=0, tiled=True)]
  transfers between devices with their start and end apart: 28 -> 28, of which waited for: 9 -> 7; matrix products, arithmetic and copies ran while one was open for 2% -> 1% of each run, Pallas kernels for 25% -> 26%
where the time goes in v1:
time: 114 us; the launch traced here: 113 us
  starting transfers between devices  54.9 us (48%)
  Pallas kernels  33.7 us (30%)
  waiting for transfers between devices  20.3 us (18%)
  local copies, waits for them, and re-layouts  2.63 us (2%)
  other arithmetic  1.44 us (1%)
    ppermute x12, starting transfers between devices, partner(): return lax.ppermute(array, 'tm', [(i, i ^ bits) for i in range(N_TM)])  25.4 us
    ppermute x14, starting transfers between devices, z_shift(): return lax.ppermute(array, 'tm', pairs)  22.2 us
    ppermute x12, waiting for transfers between devices, partner(): return lax.ppermute(array, 'tm', [(i, i ^ bits) for i in range(N_TM)])  16.3 us
    pallas_call x3, Pallas kernels, step_of(): call(functools.partial(attend_step, step), STATE, 2, 8, 2.5)  8.15 us
    pallas_call x1, Pallas kernels, on_device(): call(functools.partial(scan_inside, True), wide, 2, 1, 4, [pltpu.VMEM((2,...  4.38 us
    pallas_call x2, Pallas kernels, on_device(): call(functools.partial(attend_last, u), (piece, piece), 2, 6, 2)  4.24 us
    all_to_all x1, waiting for transfers between devices, on_device(): lax.all_to_all(sent, 'space', split_axis=0, concat_axis=0, tiled=True)  4.02 us
    all_to_all x1, starting transfers between devices, on_device(): lax.all_to_all(sent, 'space', split_axis=0, concat_axis=0, tiled=True)  3.68 us
  transfers between devices with their start and end apart: 28, of which 7 were waited for; matrix products, arithmetic and copies ran while one was open for 1% of the time, Pallas kernels for 26%

profile of v1, /device:TPU:1, one launch (start us, length us, event | category | flops | bytes accessed | tf_op | source)
XLA Modules:
  0.0 113.3 jit_solution(126200078365549224)
XLA Ops:
  0.0 0.6 pad_add_fusion.ids
  0.6 2.4 %head_groups.1 = (bf16[3,128,384]{2,1,0:T(8,128)(2,1)}, bf16[3,128,384]{2,1,0:T(8,128)(2,1)}, bf16[3,128,384]{2,1,0:T(8,128)(2,1)}, bf16[3,128,384]{2,1,0:T(8,128)(2,1)}) custom-call(s32[4]{0:T(128)} %pad_add_fusion.ids, bf16[128,1536]{1,0:T(8,128)(2,1)} %q_ref.1, bf16[128,1536]{1,0:T(8,128)(2,1)} %k_ref.1, bf16[128,1536]{1,0:T(8,128)(2,1)} %v_ref.1), custom_call_target="tpu_custom_call" | custom-call | flops 1100000 | bytes 3000 | tf_op jit(solution)/shard_map/head_groups/pallas_call | solution.py:489
  3.0 3.2 %collective-permute-start = (bf16[3,128,384]{2,1,0:T(8,128)(2,1)}, bf16[3,128,384]{2,1,0:T(8,128)(2,1)S(1)}, u32[]{:S(2)}, u32[]{:S(2)}) collective-permute-start(bf16[3,128,384]{2,1,0:T(8,128)(2,1)} %get-tuple-element.79), channel_id=1, source_target_pairs={{0,8},{8,0},{16,24},{24,16},{32,40},{40,32},{48,56},{56,48},{64,72... | collective-permute-start | bytes 884744 | tf_op jit(solution)/shard_map/ppermute | solution.py:479
  6.2 1.0 collective-permute-start.4
  7.2 2.1 %collective-permute-start.5 = (bf16[3,128,384]{2,1,0:T(8,128)(2,1)}, bf16[3,128,384]{2,1,0:T(8,128)(2,1)S(1)}, u32[]{:S(2)}, u32[]{:S(2)}) collective-permute-start(bf16[3,128,384]{2,1,0:T(8,128)(2,1)} %get-tuple-element.94), channel_id=1, source_target_pairs={{0,136},{8,128},{16,152},{24,144},{32,168},{40,160},{48,184},{56,1... | collective-permute-start | bytes 884744 | tf_op jit(solution)/shard_map/ppermute | solution.py:479
  9.3 2.0 %scan_pack.1 = bf16[8,128,384]{2,1,0:T(8,128)(2,1)} custom-call(bf16[128,1536]{1,0:T(8,128)(2,1)} %x_ref, bf16[128,128]{1,0:T(8,128)(2,1)} %bc_ref.1, bf16[24,128]{1,0:T(8,128)(2,1)} %log_ref.1), custom_call_target="tpu_custom_call" | custom-call | flops 1650000 | bytes 4500 | tf_op jit(solution)/shard_map/scan_pack/pallas_call | solution.py:496
  11.3 3.7 %all-to-all-start = ((bf16[8,128,384]{2,1,0:T(8,128)(2,1)}), bf16[8,128,384]{2,1,0:T(8,128)(2,1)S(1)}, u32[]{:S(2)}, u32[]{:S(2)}) async-start(bf16[8,128,384]{2,1,0:T(8,128)(2,1)} %scan_pack.1), calls=%async_computation | async-start | bytes 1572864 | tf_op jit(solution)/shard_map/all_to_all | solution.py:499
  15.1 5.5 %collective-permute-start.6 = (bf16[2,2,128,384]{3,2,1,0:T(8,128)(2,1)S(1)}, bf16[2,2,128,384]{3,2,1,0:T(8,128)(2,1)}, u32[]{:S(2)}, u32[]{:S(2)}) collective-permute-start(bf16[2,2,128,384]{3,2,1,0:T(8,128)(2,1)S(1)} %pad_maximum_fusion), channel_id=1, source_target_pairs={{0,112},{8,120},{16,0},{24,8},{32,16},{40,24},{48,32},{56,40},{64,... | collective-permute-start | bytes 1179656 | tf_op jit(solution)/shard_map/ppermute | solution.py:475
  20.6 3.0 %collective-permute-done.5.both = bf16[3,128,384]{2,1,0:T(8,128)(2,1)S(1)} collective-permute-done((bf16[3,128,384]{2,1,0:T(8,128)(2,1)}, bf16[3,128,384]{2,1,0:T(8,128)(2,1)S(1)}, u32[]{:S(2)}, u32[]{:S(2)}) %collective-permute-start.5) | collective-permute-done | bytes 294944 | tf_op jit(solution)/shard_map/ppermute | solution.py:479
  23.6 0.8 pad_maximum_fusion.1
  24.4 3.6 %collective-permute-start.8 = (bf16[2,2,128,384]{3,2,1,0:T(8,128)(2,1)}, bf16[2,2,128,384]{3,2,1,0:T(8,128)(2,1)}, u32[]{:S(2)}, u32[]{:S(2)}) collective-permute-start(bf16[2,2,128,384]{3,2,1,0:T(8,128)(2,1)} %pad_maximum_fusion.1), channel_id=1, source_target_pairs={{0,112},{8,120},{16,0},{24,8},{32,16},{40,24},{48,32},{56,40},{64,... | collective-permute-start | bytes 1179656 | tf_op jit(solution)/shard_map/ppermute | solution.py:475
  28.1 4.0 %all-to-all-done.in_ref = bf16[8,128,384]{2,1,0:T(8,128)(2,1)S(1)} async-done(((bf16[8,128,384]{2,1,0:T(8,128)(2,1)}), bf16[8,128,384]{2,1,0:T(8,128)(2,1)S(1)}, u32[]{:S(2)}, u32[]{:S(2)}) %all-to-all-start) | async-done | bytes 786464 | tf_op jit(solution)/shard_map/all_to_all | solution.py:499
  32.1 1.4 %scan_state.1 = (f32[8,8,128]{2,1,0:T(8,128)S(1)}, f32[8,8,128]{2,1,0:T(8,128)S(1)}, f32[144,256]{1,0:T(8,128)S(1)}, bf16[2,80,256]{2,1,0:T(8,128)(2,1)S(1)}) custom-call(s32[4]{0:T(128)S(1)} %copy-done.5, s32[32]{0:T(128)S(1)} %copy-done.8, bf16[8,128,384]{2,1,0:T(8,128)(2,1)S(1)} %all-to-all-done.in_ref), custom_call_target="tpu_custom_call" | custom-call | flops 2200000 | bytes 6000 | tf_op jit(solution)/shard_map/scan_state/pallas_call | solution.py:524
  33.5 0.9 collective-permute-start.1
  34.4 0.9 collective-permute-done.1.got_ref.core_ref
  35.3 0.6 chip_state.1
  35.9 1.7 %collective-permute-start.2 = (bf16[80,256]{1,0:T(8,128)(2,1)S(1)}, bf16[80,256]{1,0:T(8,128)(2,1)S(1)}, u32[]{:S(2)}, u32[]{:S(2)}) collective-permute-start(bf16[80,256]{1,0:T(8,128)(2,1)S(1)} %get-tuple-element.83), channel_id=1, source_target_pairs={{0,16},{8,24},{16,0},{24,8},{32,48},{40,56},{48,32},{56,40},{64,80... | collective-permute-start | bytes 122888 | tf_op jit(solution)/shard_map/ppermute | solution.py:479
  37.6 4.7 %collective-permute-start.12 = (bf16[2,2,128,384]{3,2,1,0:T(8,128)(2,1)}, bf16[2,2,128,384]{3,2,1,0:T(8,128)(2,1)S(1)}, u32[]{:S(2)}, u32[]{:S(2)}) collective-permute-start(bf16[2,2,128,384]{3,2,1,0:T(8,128)(2,1)} %collective-permute-done.6.a_up), channel_id=1, source_target_pairs={{0,112},{8,120},{16,0},{24,8},{32,16},{40,24},{48,32},{56,40},{64,... | collective-permute-start | bytes 1179656 | tf_op jit(solution)/shard_map/ppermute | solution.py:475
  42.3 2.2 %scan_inside.2.y_ref = f32[2,1024,128]{2,1,0:T(8,128)S(1)} custom-call(s32[4]{0:T(128)S(1)} %copy-done.5, s32[32]{0:T(128)S(1)} %copy-done.8, bf16[8,128,384]{2,1,0:T(8,128)(2,1)S(1)} %all-to-all-done.in_ref), custom_call_target="tpu_custom_call" | custom-call | flops 2200000 | bytes 6000 | tf_op jit(solution)/shard_map/scan_inside/pallas_call | solution.py:543
  45.2 1.6 %attend_own.1 = (f32[2,8,256]{2,1,0:T(8,128)S(1)}, f32[2,8,256]{2,1,0:T(8,128)S(1)}, f32[2,3,128,256]{3,2,1,0:T(8,128)S(1)}, bf16[2,2,128,384]{3,2,1,0:T(8,128)(2,1)S(1)}) custom-call(s32[4]{0:T(128)S(1)} %copy-done.5, s32[32,32]{1,0:T(8,128)S(1)} %copy-done.4, bf16[3,128,384]{2,1,0:T(8,128)(2,1)S(1)} %copy-done.1, ...), custom_call_target="tpu_custom_call" | custom-call | flops 2200000 | bytes 6000 | tf_op jit(solution)/shard_map/attend_own/pallas_call | solution.py:554
  46.9 2.8 %collective-permute-start.14 = (bf16[2,2,128,384]{3,2,1,0:T(8,128)(2,1)}, bf16[2,2,128,384]{3,2,1,0:T(8,128)(2,1)}, u32[]{:S(2)}, u32[]{:S(2)}) collective-permute-start(bf16[2,2,128,384]{3,2,1,0:T(8,128)(2,1)} %collective-permute-done.8.b_up), channel_id=1, source_target_pairs={{0,112},{8,120},{16,0},{24,8},{32,16},{40,24},{48,32},{56,40},{64,... | collective-permute-start | bytes 1179656 | tf_op jit(solution)/shard_map/ppermute | solution.py:475
  49.6 2.8 %attend_step.3 = (f32[2,8,256]{2,1,0:T(8,128)S(1)}, f32[2,8,256]{2,1,0:T(8,128)S(1)}, f32[2,3,128,256]{3,2,1,0:T(8,128)S(1)}) custom-call(s32[4]{0:T(128)S(1)} %copy-done.5, s32[32,32]{1,0:T(8,128)S(1)} %copy-done.4, bf16[2,2,128,384]{3,2,1,0:T(8,128)(2,1)S(1)} %get-tuple-element.95.q_ref, bf16[2,2,128,384]{3,2,1,0:T(8,128)(2,1)} %collective-permute-done.6.a_up, ...), custom_call_target="tpu_custom_call" | custom-call | flops 2750000 | bytes 7500 | tf_op jit(solution)/shard_map/attend_step/pallas_call | solution.py:514
  52.4 7.3 %collective-permute-done.3.got_ref = bf16[80,256]{1,0:T(8,128)(2,1)S(1)} collective-permute-done((bf16[80,256]{1,0:T(8,128)(2,1)S(1)}, bf16[80,256]{1,0:T(8,128)(2,1)S(1)}, u32[]{:S(2)}, u32[]{:S(2)}) %collective-permute-start.3) | collective-permute-done | bytes 40992 | tf_op jit(solution)/shard_map/ppermute | solution.py:479
  59.7 0.6 grow.4
  60.3 3.6 %collective-permute-start.10 = (bf16[80,256]{1,0:T(8,128)(2,1)S(1)}, bf16[80,256]{1,0:T(8,128)(2,1)S(1)}, u32[]{:S(2)}, u32[]{:S(2)}) collective-permute-start(bf16[80,256]{1,0:T(8,128)(2,1)S(1)} %get-tuple-element.107), channel_id=1, source_target_pairs={{0,112},{8,120},{16,96},{24,104},{32,80},{40,88},{48,64},{56,72},{... | collective-permute-start | bytes 122888 | tf_op jit(solution)/shard_map/ppermute | solution.py:479
  64.0 4.4 %scan_inside.3.z_ref = f32[2,1024,128]{2,1,0:T(8,128)S(1)} custom-call(s32[4]{0:T(128)S(1)} %copy-done.5, s32[32]{0:T(128)S(1)} %copy-done.8, bf16[8,128,384]{2,1,0:T(8,128)(2,1)S(1)} %all-to-all-done.in_ref), custom_call_target="tpu_custom_call" | custom-call | flops 4400000 | bytes 12000 | tf_op jit(solution)/shard_map/scan_inside/pallas_call | solution.py:566
  68.4 1.2 %grow.5 = (f32[72,256]{1,0:T(8,128)S(1)}, f32[72,256]{1,0:T(8,128)}, bf16[80,256]{1,0:T(8,128)(2,1)S(1)}) custom-call(s32[4]{0:T(128)S(1)} %copy-done.5, bf16[80,256]{1,0:T(8,128)(2,1)S(1)} %collective-permute-done.10.got_ref, f32[72,256]{1,0:T(8,128)S(1)} %get-tuple-element.113.total_in, f32[72,256]{1,0:T(8,128)S(1)} %get-tuple-element.114.rest_0_), custom_call_target="tpu_custom_call" | custom-call | flops 550000 | bytes 1500 | tf_op jit(solution)/shard_map/grow/pallas_call | solution.py:575
  69.6 1.4 %collective-permute-start.20 = (bf16[2,2,128,384]{3,2,1,0:T(8,128)(2,1)S(1)}, bf16[2,2,128,384]{3,2,1,0:T(8,128)(2,1)}, u32[]{:S(2)}, u32[]{:S(2)}) collective-permute-start(bf16[2,2,128,384]{3,2,1,0:T(8,128)(2,1)S(1)} %collective-permute-done.15.b_down), channel_id=1, source_target_pairs={{0,16},{8,24},{16,32},{24,40},{32,48},{40,56},{48,64},{56,72},{64,... | collective-permute-start | bytes 1179656 | tf_op jit(solution)/shard_map/ppermute | solution.py:475
  71.0 1.7 %collective-permute-start.11 = (bf16[80,256]{1,0:T(8,128)(2,1)S(1)}, bf16[80,256]{1,0:T(8,128)(2,1)S(1)}, u32[]{:S(2)}, u32[]{:S(2)}) collective-permute-start(bf16[80,256]{1,0:T(8,128)(2,1)S(1)} %get-tuple-element.115), channel_id=1, source_target_pairs={{0,128},{8,136},{16,144},{24,152},{32,160},{40,168},{48,176},{56,1... | collective-permute-start | bytes 122888 | tf_op jit(solution)/shard_map/ppermute | solution.py:479
  72.7 0.8 collective-permute-start.18
  73.5 1.9 %collective-permute-start.19 = (bf16[2,2,128,384]{3,2,1,0:T(8,128)(2,1)}, bf16[2,2,128,384]{3,2,1,0:T(8,128)(2,1)}, u32[]{:S(2)}, u32[]{:S(2)}) collective-permute-start(bf16[2,2,128,384]{3,2,1,0:T(8,128)(2,1)} %collective-permute-done.14.b_up), channel_id=1, source_target_pairs={{0,112},{8,120},{16,0},{24,8},{32,16},{40,24},{48,32},{56,40},{64,... | collective-permute-start | bytes 1179656 | tf_op jit(solution)/shard_map/ppermute | solution.py:475
  75.4 2.6 %attend_step.4 = (f32[2,8,256]{2,1,0:T(8,128)S(1)}, f32[2,8,256]{2,1,0:T(8,128)S(1)}, f32[2,3,128,256]{3,2,1,0:T(8,128)S(1)}) custom-call(s32[4]{0:T(128)S(1)} %copy-done.5, s32[32,32]{1,0:T(8,128)S(1)} %copy-done.4, bf16[2,2,128,384]{3,2,1,0:T(8,128)(2,1)S(1)} %get-tuple-element.95.q_ref, bf16[2,2,128,384]{3,2,1,0:T(8,128)(2,1)S(1)} %collective-permute-done.12.a_up, ...), custom_call_target="tpu_custom_call" | custom-call | flops 2750000 | bytes 7500 | tf_op jit(solution)/shard_map/attend_step/pallas_call | solution.py:514
  78.0 0.9 copy-done.2
  79.8 1.2 %collective-permute-start.22 = (bf16[2,2,128,384]{3,2,1,0:T(8,128)(2,1)}, bf16[2,2,128,384]{3,2,1,0:T(8,128)(2,1)}, u32[]{:S(2)}, u32[]{:S(2)}) collective-permute-start(bf16[2,2,128,384]{3,2,1,0:T(8,128)(2,1)} %collective-permute-done.20.b_down), channel_id=1, source_target_pairs={{0,16},{8,24},{16,32},{24,40},{32,48},{40,56},{48,64},{56,72},{64,... | collective-permute-start | bytes 1179656 | tf_op jit(solution)/shard_map/ppermute | solution.py:475
  81.0 6.4 %collective-permute-start.16 = (bf16[64,256]{1,0:T(8,128)(2,1)S(1)}, bf16[64,256]{1,0:T(8,128)(2,1)S(1)}, u32[]{:S(2)}, u32[]{:S(2)}) collective-permute-start(bf16[64,256]{1,0:T(8,128)(2,1)S(1)} %last_before.1.before_ref), channel_id=1, source_target_pairs={{0,8},{8,0},{16,24},{24,16},{32,40},{40,32},{48,56},{56,48},{64,72... | collective-permute-start | bytes 98312 | tf_op jit(solution)/shard_map/ppermute | solution.py:479
  87.4 0.8 dynamic_slice.3
  88.3 2.4 %scan_finish.1 = bf16[8,192,128]{2,1,0:T(8,128)(2,1)S(1)} custom-call(s32[4]{0:T(128)S(1)} %copy-done.5, bf16[8,128,384]{2,1,0:T(8,128)(2,1)S(1)} %all-to-all-done.in_ref, f32[2,1024,128]{2,1,0:T(8,128)S(1)} %scan_inside.2.y_ref, f32[2,1024,128]{2,1,0:T(8,128)S(1)} %scan_inside.3.z_ref, f32[8,8,128]{2,1,0:T(8,128)S(1)} %get-tuple-element.110.row_ref, ...), custom_call_target="tpu_custom_call" | custom-call | flops 3300000 | bytes 9000 | tf_op jit(solution)/shard_map/scan_finish/pallas_call | solution.py:592
  90.7 0.7 copy-done
  91.5 3.6 %all-to-all-start.1 = ((bf16[8,192,128]{2,1,0:T(8,128)(2,1)}), bf16[8,192,128]{2,1,0:T(8,128)(2,1)S(1)}, u32[]{:S(2)}, u32[]{:S(2)}) async-start(bf16[8,192,128]{2,1,0:T(8,128)(2,1)} %copy-done), calls=%async_computation.1 | async-start | bytes 786432 | tf_op jit(solution)/shard_map/all_to_all | solution.py:604
  95.1 2.8 %attend_step.5 = (f32[2,8,256]{2,1,0:T(8,128)S(1)}, f32[2,8,256]{2,1,0:T(8,128)S(1)}, f32[2,3,128,256]{3,2,1,0:T(8,128)S(1)}) custom-call(s32[4]{0:T(128)S(1)} %copy-done.5, s32[32,32]{1,0:T(8,128)S(1)} %copy-done.4, bf16[2,2,128,384]{3,2,1,0:T(8,128)(2,1)S(1)} %get-tuple-element.95.q_ref, bf16[2,2,128,384]{3,2,1,0:T(8,128)(2,1)} %collective-permute-done.17.a_up, ...), custom_call_target="tpu_custom_call" | custom-call | flops 2750000 | bytes 7500 | tf_op jit(solution)/shard_map/attend_step/pallas_call | solution.py:514
  97.9 2.1 %attend_last.2 = (bf16[128,384]{1,0:T(8,128)(2,1)S(1)}, bf16[128,384]{1,0:T(8,128)(2,1)S(1)}) custom-call(s32[4]{0:T(128)S(1)} %copy-done.5, s32[32,32]{1,0:T(8,128)S(1)} %copy-done.4, bf16[2,2,128,384]{3,2,1,0:T(8,128)(2,1)S(1)} %get-tuple-element.95.q_ref, bf16[2,2,128,384]{3,2,1,0:T(8,128)(2,1)} %collective-permute-done.21.a_ref, ...), custom_call_target="tpu_custom_call" | custom-call | flops 2200000 | bytes 6000 | tf_op jit(solution)/shard_map/attend_last/pallas_call | solution.py:610
  100.0 2.1 %attend_last.3 = (bf16[128,384]{1,0:T(8,128)(2,1)S(1)}, bf16[128,384]{1,0:T(8,128)(2,1)S(1)}) custom-call(s32[4]{0:T(128)S(1)} %copy-done.5, s32[32,32]{1,0:T(8,128)S(1)} %copy-done.4, bf16[2,2,128,384]{3,2,1,0:T(8,128)(2,1)S(1)} %get-tuple-element.95.q_ref, bf16[2,2,128,384]{3,2,1,0:T(8,128)(2,1)} %collective-permute-done.21.a_ref, ...), custom_call_target="tpu_custom_call" | custom-call | flops 2200000 | bytes 6000 | tf_op jit(solution)/shard_map/attend_last/pallas_call | solution.py:610
  102.2 1.5 %collective-permute-start.23 = (bf16[128,384]{1,0:T(8,128)(2,1)S(1)}, bf16[128,384]{1,0:T(8,128)(2,1)S(1)}, u32[]{:S(2)}, u32[]{:S(2)}) collective-permute-start(bf16[128,384]{1,0:T(8,128)(2,1)S(1)} %get-tuple-element.150), channel_id=1, source_target_pairs={{0,8},{8,0},{16,24},{24,16},{32,40},{40,32},{48,56},{56,48},{64,72... | collective-permute-start | bytes 294920 | tf_op jit(solution)/shard_map/ppermute | solution.py:479
  103.6 1.8 %collective-permute-start.24 = (bf16[128,384]{1,0:T(8,128)(2,1)S(1)}, bf16[128,384]{1,0:T(8,128)(2,1)S(1)}, u32[]{:S(2)}, u32[]{:S(2)}) collective-permute-start(bf16[128,384]{1,0:T(8,128)(2,1)S(1)} %get-tuple-element.151), channel_id=1, source_target_pairs={{0,128},{8,136},{16,144},{24,152},{32,160},{40,168},{48,176},{56,1... | collective-permute-start | bytes 294920 | tf_op jit(solution)/shard_map/ppermute | solution.py:479
  105.4 1.5 %collective-permute-start.25 = (bf16[128,384]{1,0:T(8,128)(2,1)S(1)}, bf16[128,384]{1,0:T(8,128)(2,1)S(1)}, u32[]{:S(2)}, u32[]{:S(2)}) collective-permute-start(bf16[128,384]{1,0:T(8,128)(2,1)S(1)} %get-tuple-element.152), channel_id=1, source_target_pairs={{0,136},{8,128},{16,152},{24,144},{32,168},{40,160},{48,184},{56,1... | collective-permute-start | bytes 294920 | tf_op jit(solution)/shard_map/ppermute | solution.py:479
  106.9 2.6 %collective-permute-done.24.rest_2_ = bf16[128,384]{1,0:T(8,128)(2,1)S(1)} collective-permute-done((bf16[128,384]{1,0:T(8,128)(2,1)S(1)}, bf16[128,384]{1,0:T(8,128)(2,1)S(1)}, u32[]{:S(2)}, u32[]{:S(2)}) %collective-permute-start.24) | collective-permute-done | bytes 98336 | tf_op jit(solution)/shard_map/ppermute | solution.py:479
  109.5 2.4 %collective-permute-done.25.rest_3_ = bf16[128,384]{1,0:T(8,128)(2,1)S(1)} collective-permute-done((bf16[128,384]{1,0:T(8,128)(2,1)S(1)}, bf16[128,384]{1,0:T(8,128)(2,1)S(1)}, u32[]{:S(2)}, u32[]{:S(2)}) %collective-permute-start.25) | collective-permute-done | bytes 98336 | tf_op jit(solution)/shard_map/ppermute | solution.py:479
  111.9 1.5 %add_up.1 = bf16[128,1536]{1,0:T(8,128)(2,1)} custom-call(s32[4]{0:T(128)S(1)} %copy-done.5, bf16[8,192,128]{2,1,0:T(8,128)(2,1)S(1)} %all-to-all-done.1.scan_ref, bf16[128,384]{1,0:T(8,128)(2,1)S(1)} %get-tuple-element.149.rest_0_, bf16[128,384]{1,0:T(8,128)(2,1)S(1)} %collective-permute-done.23.rest_1_, ...), custom_call_target="tpu_custom_call" | custom-call | flops 1650000 | bytes 4500 | tf_op jit(solution)/shard_map/add_up/pallas_call | solution.py:620
  (51 shorter events, 2.0 us)
Async XLA Ops:
  3.0 6.4 %collective-permute-start = (bf16[3,128,384]{2,1,0:T(8,128)(2,1)}, bf16[3,128,384]{2,1,0:T(8,128)(2,1)S(1)}, u32[]{:S(2)}, u32[]{:S(2)}) collective-permute-start(bf16[3,128,384]{2,1,0:T(8,128)(2,1)} %get-tuple-element.79), channel_id=1, source_target_pairs={{0,8},{8,0},{16,24},{24,16},{32,40},{40,32},{48,56},{56,48},{64,72... | collective-permute-start | bytes 884744 | tf_op jit(solution)/shard_map/ppermute | solution.py:479
  6.2 17.4 %collective-permute-start.4 = (bf16[3,128,384]{2,1,0:T(8,128)(2,1)}, bf16[3,128,384]{2,1,0:T(8,128)(2,1)S(1)}, u32[]{:S(2)}, u32[]{:S(2)}) collective-permute-start(bf16[3,128,384]{2,1,0:T(8,128)(2,1)} %get-tuple-element.93), channel_id=1, source_target_pairs={{0,128},{8,136},{16,144},{24,152},{32,160},{40,168},{48,176},{56,1... | collective-permute-start | bytes 884744 | tf_op jit(solution)/shard_map/ppermute | solution.py:479
  7.2 16.4 %collective-permute-start.5 = (bf16[3,128,384]{2,1,0:T(8,128)(2,1)}, bf16[3,128,384]{2,1,0:T(8,128)(2,1)S(1)}, u32[]{:S(2)}, u32[]{:S(2)}) collective-permute-start(bf16[3,128,384]{2,1,0:T(8,128)(2,1)} %get-tuple-element.94), channel_id=1, source_target_pairs={{0,136},{8,128},{16,152},{24,144},{32,168},{40,160},{48,184},{56,1... | collective-permute-start | bytes 884744 | tf_op jit(solution)/shard_map/ppermute | solution.py:479
  11.3 3.7 %copy-start.1 = (bf16[3,128,384]{2,1,0:T(8,128)(2,1)S(1)}, bf16[3,128,384]{2,1,0:T(8,128)(2,1)}, u32[]{:S(2)}) copy-start(bf16[3,128,384]{2,1,0:T(8,128)(2,1)} %get-tuple-element.91.own) | copy-start | bytes 884740
  11.3 20.8 %all-to-all-start = ((bf16[8,128,384]{2,1,0:T(8,128)(2,1)}), bf16[8,128,384]{2,1,0:T(8,128)(2,1)S(1)}, u32[]{:S(2)}, u32[]{:S(2)}) async-start(bf16[8,128,384]{2,1,0:T(8,128)(2,1)} %scan_pack.1), calls=%async_computation | async-start | bytes 1572864 | tf_op jit(solution)/shard_map/all_to_all | solution.py:499
  15.1 22.5 %collective-permute-start.6 = (bf16[2,2,128,384]{3,2,1,0:T(8,128)(2,1)S(1)}, bf16[2,2,128,384]{3,2,1,0:T(8,128)(2,1)}, u32[]{:S(2)}, u32[]{:S(2)}) collective-permute-start(bf16[2,2,128,384]{3,2,1,0:T(8,128)(2,1)S(1)} %pad_maximum_fusion), channel_id=1, source_target_pairs={{0,112},{8,120},{16,0},{24,8},{32,16},{40,24},{48,32},{56,40},{64,... | collective-permute-start | bytes 1179656 | tf_op jit(solution)/shard_map/ppermute | solution.py:475
  20.6 21.7 %collective-permute-start.7 = (bf16[2,2,128,384]{3,2,1,0:T(8,128)(2,1)S(1)}, bf16[2,2,128,384]{3,2,1,0:T(8,128)(2,1)}, u32[]{:S(2)}, u32[]{:S(2)}) collective-permute-start(bf16[2,2,128,384]{3,2,1,0:T(8,128)(2,1)S(1)} %pad_maximum_fusion), channel_id=1, source_target_pairs={{0,16},{8,24},{16,32},{24,40},{32,48},{40,56},{48,64},{56,72},{64,... | collective-permute-start | bytes 1179656 | tf_op jit(solution)/shard_map/ppermute | solution.py:475
  23.6 8.5 %copy-start.5 = (s32[4]{0:T(128)S(1)}, s32[4]{0:T(128)}, u32[]{:S(2)}) copy-start(s32[4]{0:T(128)} %pad_add_fusion.ids) | copy-start | bytes 52
  23.6 8.5 %copy-start.8 = (s32[32]{0:T(128)S(1)}, s32[32]{0:T(128)}, u32[]{:S(2)}) copy-start(s32[32]{0:T(128)} %order_ref.5) | copy-start | bytes 388
  24.4 22.4 %collective-permute-start.8 = (bf16[2,2,128,384]{3,2,1,0:T(8,128)(2,1)}, bf16[2,2,128,384]{3,2,1,0:T(8,128)(2,1)}, u32[]{:S(2)}, u32[]{:S(2)}) collective-permute-start(bf16[2,2,128,384]{3,2,1,0:T(8,128)(2,1)} %pad_maximum_fusion.1), channel_id=1, source_target_pairs={{0,112},{8,120},{16,0},{24,8},{32,16},{40,24},{48,32},{56,40},{64,... | collective-permute-start | bytes 1179656 | tf_op jit(solution)/shard_map/ppermute | solution.py:475
  28.1 18.8 %collective-permute-start.9 = (bf16[2,2,128,384]{3,2,1,0:T(8,128)(2,1)}, bf16[2,2,128,384]{3,2,1,0:T(8,128)(2,1)}, u32[]{:S(2)}, u32[]{:S(2)}) collective-permute-start(bf16[2,2,128,384]{3,2,1,0:T(8,128)(2,1)} %pad_maximum_fusion.1), channel_id=1, source_target_pairs={{0,16},{8,24},{16,32},{24,40},{32,48},{40,56},{48,64},{56,72},{64,... | collective-permute-start | bytes 1179656 | tf_op jit(solution)/shard_map/ppermute | solution.py:475
  33.5 2.4 %copy-start.6 = (f32[8,8,128]{2,1,0:T(8,128)}, f32[8,8,128]{2,1,0:T(8,128)S(1)}, u32[]{:S(2)}) copy-start(f32[8,8,128]{2,1,0:T(8,128)S(1)} %get-tuple-element.111.col_ref) | copy-start | bytes 98308
  33.5 1.8 %collective-permute-start.1 = (bf16[2,80,256]{2,1,0:T(8,128)(2,1)S(1)}, bf16[2,80,256]{2,1,0:T(8,128)(2,1)S(1)}, u32[]{:S(2)}, u32[]{:S(2)}) collective-permute-start(bf16[2,80,256]{2,1,0:T(8,128)(2,1)S(1)} %get-tuple-element.82), channel_id=1, source_target_pairs={{0,8},{8,0},{16,24},{24,16},{32,40},{40,32},{48,56},{56,48},{64,72... | collective-permute-start | bytes 245768 | tf_op jit(solution)/shard_map/ppermute | solution.py:479
  35.9 8.6 %collective-permute-start.2 = (bf16[80,256]{1,0:T(8,128)(2,1)S(1)}, bf16[80,256]{1,0:T(8,128)(2,1)S(1)}, u32[]{:S(2)}, u32[]{:S(2)}) collective-permute-start(bf16[80,256]{1,0:T(8,128)(2,1)S(1)} %get-tuple-element.83), channel_id=1, source_target_pairs={{0,16},{8,24},{16,0},{24,8},{32,48},{40,56},{48,32},{56,40},{64,80... | collective-permute-start | bytes 122888 | tf_op jit(solution)/shard_map/ppermute | solution.py:479
  37.6 26.3 %collective-permute-start.12 = (bf16[2,2,128,384]{3,2,1,0:T(8,128)(2,1)}, bf16[2,2,128,384]{3,2,1,0:T(8,128)(2,1)S(1)}, u32[]{:S(2)}, u32[]{:S(2)}) collective-permute-start(bf16[2,2,128,384]{3,2,1,0:T(8,128)(2,1)} %collective-permute-done.6.a_up), channel_id=1, source_target_pairs={{0,112},{8,120},{16,0},{24,8},{32,16},{40,24},{48,32},{56,40},{64,... | collective-permute-start | bytes 1179656 | tf_op jit(solution)/shard_map/ppermute | solution.py:475
  42.3 21.6 %collective-permute-start.13 = (bf16[2,2,128,384]{3,2,1,0:T(8,128)(2,1)}, bf16[2,2,128,384]{3,2,1,0:T(8,128)(2,1)}, u32[]{:S(2)}, u32[]{:S(2)}) collective-permute-start(bf16[2,2,128,384]{3,2,1,0:T(8,128)(2,1)} %collective-permute-done.7.a_down), channel_id=1, source_target_pairs={{0,16},{8,24},{16,32},{24,40},{32,48},{40,56},{48,64},{56,72},{64,... | collective-permute-start | bytes 1179656 | tf_op jit(solution)/shard_map/ppermute | solution.py:475
  44.5 0.7 copy-start.4
  46.9 22.7 %collective-permute-start.14 = (bf16[2,2,128,384]{3,2,1,0:T(8,128)(2,1)}, bf16[2,2,128,384]{3,2,1,0:T(8,128)(2,1)}, u32[]{:S(2)}, u32[]{:S(2)}) collective-permute-start(bf16[2,2,128,384]{3,2,1,0:T(8,128)(2,1)} %collective-permute-done.8.b_up), channel_id=1, source_target_pairs={{0,112},{8,120},{16,0},{24,8},{32,16},{40,24},{48,32},{56,40},{64,... | collective-permute-start | bytes 1179656 | tf_op jit(solution)/shard_map/ppermute | solution.py:475
  49.6 20.0 %collective-permute-start.15 = (bf16[2,2,128,384]{3,2,1,0:T(8,128)(2,1)}, bf16[2,2,128,384]{3,2,1,0:T(8,128)(2,1)S(1)}, u32[]{:S(2)}, u32[]{:S(2)}) collective-permute-start(bf16[2,2,128,384]{3,2,1,0:T(8,128)(2,1)} %collective-permute-done.9.b_down), channel_id=1, source_target_pairs={{0,16},{8,24},{16,32},{24,40},{32,48},{40,56},{48,64},{56,72},{64,... | collective-permute-start | bytes 1179656 | tf_op jit(solution)/shard_map/ppermute | solution.py:475
  49.6 10.1 %collective-permute-start.3 = (bf16[80,256]{1,0:T(8,128)(2,1)S(1)}, bf16[80,256]{1,0:T(8,128)(2,1)S(1)}, u32[]{:S(2)}, u32[]{:S(2)}) collective-permute-start(bf16[80,256]{1,0:T(8,128)(2,1)S(1)} %get-tuple-element.88), channel_id=1, source_target_pairs={{0,32},{8,40},{16,48},{24,56},{32,0},{40,8},{48,16},{56,24},{64,96... | collective-permute-start | bytes 122888 | tf_op jit(solution)/shard_map/ppermute | solution.py:479
  60.3 8.1 %collective-permute-start.10 = (bf16[80,256]{1,0:T(8,128)(2,1)S(1)}, bf16[80,256]{1,0:T(8,128)(2,1)S(1)}, u32[]{:S(2)}, u32[]{:S(2)}) collective-permute-start(bf16[80,256]{1,0:T(8,128)(2,1)S(1)} %get-tuple-element.107), channel_id=1, source_target_pairs={{0,112},{8,120},{16,96},{24,104},{32,80},{40,88},{48,64},{56,72},{... | collective-permute-start | bytes 122888 | tf_op jit(solution)/shard_map/ppermute | solution.py:479
  63.9 15.6 %collective-permute-start.17 = (bf16[2,2,128,384]{3,2,1,0:T(8,128)(2,1)S(1)}, bf16[2,2,128,384]{3,2,1,0:T(8,128)(2,1)}, u32[]{:S(2)}, u32[]{:S(2)}) collective-permute-start(bf16[2,2,128,384]{3,2,1,0:T(8,128)(2,1)S(1)} %collective-permute-done.12.a_up), channel_id=1, source_target_pairs={{0,112},{8,120},{16,0},{24,8},{32,16},{40,24},{48,32},{56,40},{64,... | collective-permute-start | bytes 1179656 | tf_op jit(solution)/shard_map/ppermute | solution.py:475
  69.6 9.9 %collective-permute-start.20 = (bf16[2,2,128,384]{3,2,1,0:T(8,128)(2,1)S(1)}, bf16[2,2,128,384]{3,2,1,0:T(8,128)(2,1)}, u32[]{:S(2)}, u32[]{:S(2)}) collective-permute-start(bf16[2,2,128,384]{3,2,1,0:T(8,128)(2,1)S(1)} %collective-permute-done.15.b_down), channel_id=1, source_target_pairs={{0,16},{8,24},{16,32},{24,40},{32,48},{40,56},{48,64},{56,72},{64,... | collective-permute-start | bytes 1179656 | tf_op jit(solution)/shard_map/ppermute | solution.py:475
  71.0 7.9 %collective-permute-start.11 = (bf16[80,256]{1,0:T(8,128)(2,1)S(1)}, bf16[80,256]{1,0:T(8,128)(2,1)S(1)}, u32[]{:S(2)}, u32[]{:S(2)}) collective-permute-start(bf16[80,256]{1,0:T(8,128)(2,1)S(1)} %get-tuple-element.115), channel_id=1, source_target_pairs={{0,128},{8,136},{16,144},{24,152},{32,160},{40,168},{48,176},{56,1... | collective-permute-start | bytes 122888 | tf_op jit(solution)/shard_map/ppermute | solution.py:479
  72.7 22.4 %collective-permute-start.18 = (bf16[2,2,128,384]{3,2,1,0:T(8,128)(2,1)}, bf16[2,2,128,384]{3,2,1,0:T(8,128)(2,1)}, u32[]{:S(2)}, u32[]{:S(2)}) collective-permute-start(bf16[2,2,128,384]{3,2,1,0:T(8,128)(2,1)} %collective-permute-done.13.a_down), channel_id=1, source_target_pairs={{0,16},{8,24},{16,32},{24,40},{32,48},{40,56},{48,64},{56,72},{64,... | collective-permute-start | bytes 1179656 | tf_op jit(solution)/shard_map/ppermute | solution.py:475
  73.5 21.6 %collective-permute-start.19 = (bf16[2,2,128,384]{3,2,1,0:T(8,128)(2,1)}, bf16[2,2,128,384]{3,2,1,0:T(8,128)(2,1)}, u32[]{:S(2)}, u32[]{:S(2)}) collective-permute-start(bf16[2,2,128,384]{3,2,1,0:T(8,128)(2,1)} %collective-permute-done.14.b_up), channel_id=1, source_target_pairs={{0,112},{8,120},{16,0},{24,8},{32,16},{40,24},{48,32},{56,40},{64,... | collective-permute-start | bytes 1179656 | tf_op jit(solution)/shard_map/ppermute | solution.py:475
  78.0 0.9 copy-start.2
  79.4 8.9 %copy-start.7 = (f32[8,8,128]{2,1,0:T(8,128)S(1)}, f32[8,8,128]{2,1,0:T(8,128)}, u32[]{:S(2)}) copy-start(f32[8,8,128]{2,1,0:T(8,128)} %copy-done.6) | copy-start | bytes 98308
  79.5 18.4 %collective-permute-start.21 = (bf16[2,2,128,384]{3,2,1,0:T(8,128)(2,1)}, bf16[2,2,128,384]{3,2,1,0:T(8,128)(2,1)}, u32[]{:S(2)}, u32[]{:S(2)}) collective-permute-start(bf16[2,2,128,384]{3,2,1,0:T(8,128)(2,1)} %collective-permute-done.17.a_up), channel_id=1, source_target_pairs={{0,112},{8,120},{16,0},{24,8},{32,16},{40,24},{48,32},{56,40},{64,... | collective-permute-start | bytes 1179656 | tf_op jit(solution)/shard_map/ppermute | solution.py:475
  79.8 18.1 %collective-permute-start.22 = (bf16[2,2,128,384]{3,2,1,0:T(8,128)(2,1)}, bf16[2,2,128,384]{3,2,1,0:T(8,128)(2,1)}, u32[]{:S(2)}, u32[]{:S(2)}) collective-permute-start(bf16[2,2,128,384]{3,2,1,0:T(8,128)(2,1)} %collective-permute-done.20.b_down), channel_id=1, source_target_pairs={{0,16},{8,24},{16,32},{24,40},{32,48},{40,56},{48,64},{56,72},{64,... | collective-permute-start | bytes 1179656 | tf_op jit(solution)/shard_map/ppermute | solution.py:475
  81.0 7.3 %collective-permute-start.16 = (bf16[64,256]{1,0:T(8,128)(2,1)S(1)}, bf16[64,256]{1,0:T(8,128)(2,1)S(1)}, u32[]{:S(2)}, u32[]{:S(2)}) collective-permute-start(bf16[64,256]{1,0:T(8,128)(2,1)S(1)} %last_before.1.before_ref), channel_id=1, source_target_pairs={{0,8},{8,0},{16,24},{24,16},{32,40},{40,32},{48,56},{56,48},{64,72... | collective-permute-start | bytes 98312 | tf_op jit(solution)/shard_map/ppermute | solution.py:479
  90.7 0.7 copy-start
  91.5 3.6 %copy-start.3 = (f32[2,3,128,256]{3,2,1,0:T(8,128)S(1)}, f32[2,3,128,256]{3,2,1,0:T(8,128)}, u32[]{:S(2)}) copy-start(f32[2,3,128,256]{3,2,1,0:T(8,128)} %copy-done.2) | copy-start | bytes 2359300
  91.5 15.4 %all-to-all-start.1 = ((bf16[8,192,128]{2,1,0:T(8,128)(2,1)}), bf16[8,192,128]{2,1,0:T(8,128)(2,1)S(1)}, u32[]{:S(2)}, u32[]{:S(2)}) async-start(bf16[8,192,128]{2,1,0:T(8,128)(2,1)} %copy-done), calls=%async_computation.1 | async-start | bytes 786432 | tf_op jit(solution)/shard_map/all_to_all | solution.py:604
  102.2 4.7 %collective-permute-start.23 = (bf16[128,384]{1,0:T(8,128)(2,1)S(1)}, bf16[128,384]{1,0:T(8,128)(2,1)S(1)}, u32[]{:S(2)}, u32[]{:S(2)}) collective-permute-start(bf16[128,384]{1,0:T(8,128)(2,1)S(1)} %get-tuple-element.150), channel_id=1, source_target_pairs={{0,8},{8,0},{16,24},{24,16},{32,40},{40,32},{48,56},{56,48},{64,72... | collective-permute-start | bytes 294920 | tf_op jit(solution)/shard_map/ppermute | solution.py:479
  103.6 5.9 %collective-permute-start.24 = (bf16[128,384]{1,0:T(8,128)(2,1)S(1)}, bf16[128,384]{1,0:T(8,128)(2,1)S(1)}, u32[]{:S(2)}, u32[]{:S(2)}) collective-permute-start(bf16[128,384]{1,0:T(8,128)(2,1)S(1)} %get-tuple-element.151), channel_id=1, source_target_pairs={{0,128},{8,136},{16,144},{24,152},{32,160},{40,168},{48,176},{56,1... | collective-permute-start | bytes 294920 | tf_op jit(solution)/shard_map/ppermute | solution.py:479
  105.4 6.5 %collective-permute-start.25 = (bf16[128,384]{1,0:T(8,128)(2,1)S(1)}, bf16[128,384]{1,0:T(8,128)(2,1)S(1)}, u32[]{:S(2)}, u32[]{:S(2)}) collective-permute-start(bf16[128,384]{1,0:T(8,128)(2,1)S(1)} %get-tuple-element.152), channel_id=1, source_target_pairs={{0,136},{8,128},{16,152},{24,144},{32,168},{40,160},{48,184},{56,1... | collective-permute-start | bytes 294920 | tf_op jit(solution)/shard_map/ppermute | solution.py:479

commit v2 on v1

--- a/solution.py
+++ b/solution.py
@@ -556,13 +556,7 @@
     )(ids, tile_mask, own, from_core, from_half, from_both)
     pass_on(1, 2, flash)
     flash = step_of(1, flash)
-    other, flash = tie(other, flash)
-    before, total, walk = call(functools.partial(grow, 4), (one, one, sent), 1, 3, 0.5)(
-        ids, other, total, before
-    )
-
-    other = partner(walk, 14)
-    inside_in, _ = tie(frame_in, walk)
+    inside_in, _ = tie(frame_in, flash)
     y_col = call(
         functools.partial(scan_inside, True),
         wide,
@@ -571,7 +565,12 @@
         4,
         [pltpu.VMEM((2, 3, frame_tokens, 128), F32)],
     )(ids, col_order, inside_in)
-    other, y_col = tie(other, y_col)
+    other, flash, y_col = tie(other, flash, y_col)
+    before, total, walk = call(functools.partial(grow, 4), (one, one, sent), 1, 3, 0.5)(
+        ids, other, total, before
+    )
+
+    other = partner(walk, 14)
     before, total, walk = call(functools.partial(grow, 8), (one, one, sent), 1, 3, 0.5)(
         ids, other, total, before
     )

time: 114 us -> 111 us (0.974)
  waiting for transfers between devices: 20.3 us -> 17.5 us
    ppermute x12, waiting for transfers between devices: 16.3 us -> 13.5 us  [partner(): return lax.ppermute(array, 'tm', [(i, i ^ bits) for i in range(N_TM)])]
  transfers between devices with their start and end apart: 28 -> 28, of which waited for: 7 -> 8; matrix products, arithmetic and copies ran while one was open for 1% -> 2% of each run, Pallas kernels for 26% -> 27%
where the time goes in v2:
time: 111 us
  starting transfers between devices  54.9 us (49%)
  Pallas kernels  33.8 us (30%)
  waiting for transfers between devices  17.5 us (16%)
  local copies, waits for them, and re-layouts  2.63 us (2%)
  other arithmetic  1.44 us (1%)
    ppermute x12, starting transfers between devices, partner(): return lax.ppermute(array, 'tm', [(i, i ^ bits) for i in range(N_TM)])  25.3 us
    ppermute x14, starting transfers between devices, z_shift(): return lax.ppermute(array, 'tm', pairs)  22.3 us
    ppermute x12, waiting for transfers between devices, partner(): return lax.ppermute(array, 'tm', [(i, i ^ bits) for i in range(N_TM)])  13.5 us
    pallas_call x3, Pallas kernels, step_of(): call(functools.partial(attend_step, step), STATE, 2, 8, 2.5)  8.28 us
    pallas_call x1, Pallas kernels, on_device(): call(functools.partial(scan_inside, True), wide, 2, 1, 4, [pltpu.VMEM((2,...  4.37 us
    pallas_call x2, Pallas kernels, on_device(): call(functools.partial(attend_last, u), (piece, piece), 2, 6, 2)  4.25 us
    all_to_all x1, waiting for transfers between devices, on_device(): lax.all_to_all(sent, 'space', split_axis=0, concat_axis=0, tiled=True)  4.02 us
    all_to_all x1, starting transfers between devices, on_device(): lax.all_to_all(sent, 'space', split_axis=0, concat_axis=0, tiled=True)  3.68 us
  transfers between devices with their start and end apart: 28, of which 8 were waited for; matrix products, arithmetic and copies ran while one was open for 2% of the time, Pallas kernels for 27%

profile of v2, /device:TPU:1, one launch (start us, length us, event | category | flops | bytes accessed | tf_op | source)
XLA Modules:
  0.0 110.6 jit_solution(8671616420329091875)
XLA Ops:
  0.0 0.6 pad_add_fusion.ids
  0.6 2.4 %head_groups.1 = (bf16[3,128,384]{2,1,0:T(8,128)(2,1)}, bf16[3,128,384]{2,1,0:T(8,128)(2,1)}, bf16[3,128,384]{2,1,0:T(8,128)(2,1)}, bf16[3,128,384]{2,1,0:T(8,128)(2,1)}) custom-call(s32[4]{0:T(128)} %pad_add_fusion.ids, bf16[128,1536]{1,0:T(8,128)(2,1)} %q_ref.1, bf16[128,1536]{1,0:T(8,128)(2,1)} %k_ref.1, bf16[128,1536]{1,0:T(8,128)(2,1)} %v_ref.1), custom_call_target="tpu_custom_call" | custom-call | flops 1100000 | bytes 3000 | tf_op jit(solution)/shard_map/head_groups/pallas_call | solution.py:489
  3.0 3.2 %collective-permute-start = (bf16[3,128,384]{2,1,0:T(8,128)(2,1)}, bf16[3,128,384]{2,1,0:T(8,128)(2,1)S(1)}, u32[]{:S(2)}, u32[]{:S(2)}) collective-permute-start(bf16[3,128,384]{2,1,0:T(8,128)(2,1)} %get-tuple-element.78), channel_id=1, source_target_pairs={{0,8},{8,0},{16,24},{24,16},{32,40},{40,32},{48,56},{56,48},{64,72... | collective-permute-start | bytes 884744 | tf_op jit(solution)/shard_map/ppermute | solution.py:479
  6.2 1.0 collective-permute-start.4
  7.2 2.1 %collective-permute-start.5 = (bf16[3,128,384]{2,1,0:T(8,128)(2,1)}, bf16[3,128,384]{2,1,0:T(8,128)(2,1)S(1)}, u32[]{:S(2)}, u32[]{:S(2)}) collective-permute-start(bf16[3,128,384]{2,1,0:T(8,128)(2,1)} %get-tuple-element.93), channel_id=1, source_target_pairs={{0,136},{8,128},{16,152},{24,144},{32,168},{40,160},{48,184},{56,1... | collective-permute-start | bytes 884744 | tf_op jit(solution)/shard_map/ppermute | solution.py:479
  9.3 2.0 %scan_pack.1 = bf16[8,128,384]{2,1,0:T(8,128)(2,1)} custom-call(bf16[128,1536]{1,0:T(8,128)(2,1)} %x_ref, bf16[128,128]{1,0:T(8,128)(2,1)} %bc_ref.1, bf16[24,128]{1,0:T(8,128)(2,1)} %log_ref.1), custom_call_target="tpu_custom_call" | custom-call | flops 1650000 | bytes 4500 | tf_op jit(solution)/shard_map/scan_pack/pallas_call | solution.py:496
  11.3 3.7 %all-to-all-start = ((bf16[8,128,384]{2,1,0:T(8,128)(2,1)}), bf16[8,128,384]{2,1,0:T(8,128)(2,1)S(1)}, u32[]{:S(2)}, u32[]{:S(2)}) async-start(bf16[8,128,384]{2,1,0:T(8,128)(2,1)} %scan_pack.1), calls=%async_computation | async-start | bytes 1572864 | tf_op jit(solution)/shard_map/all_to_all | solution.py:499
  15.1 5.5 %collective-permute-start.6 = (bf16[2,2,128,384]{3,2,1,0:T(8,128)(2,1)S(1)}, bf16[2,2,128,384]{3,2,1,0:T(8,128)(2,1)}, u32[]{:S(2)}, u32[]{:S(2)}) collective-permute-start(bf16[2,2,128,384]{3,2,1,0:T(8,128)(2,1)S(1)} %pad_maximum_fusion), channel_id=1, source_target_pairs={{0,112},{8,120},{16,0},{24,8},{32,16},{40,24},{48,32},{56,40},{64,... | collective-permute-start | bytes 1179656 | tf_op jit(solution)/shard_map/ppermute | solution.py:475
  20.6 3.0 %collective-permute-done.5.both = bf16[3,128,384]{2,1,0:T(8,128)(2,1)S(1)} collective-permute-done((bf16[3,128,384]{2,1,0:T(8,128)(2,1)}, bf16[3,128,384]{2,1,0:T(8,128)(2,1)S(1)}, u32[]{:S(2)}, u32[]{:S(2)}) %collective-permute-start.5) | collective-permute-done | bytes 294944 | tf_op jit(solution)/shard_map/ppermute | solution.py:479
  23.6 0.8 pad_maximum_fusion.1
  24.4 3.6 %collective-permute-start.8 = (bf16[2,2,128,384]{3,2,1,0:T(8,128)(2,1)}, bf16[2,2,128,384]{3,2,1,0:T(8,128)(2,1)}, u32[]{:S(2)}, u32[]{:S(2)}) collective-permute-start(bf16[2,2,128,384]{3,2,1,0:T(8,128)(2,1)} %pad_maximum_fusion.1), channel_id=1, source_target_pairs={{0,112},{8,120},{16,0},{24,8},{32,16},{40,24},{48,32},{56,40},{64,... | collective-permute-start | bytes 1179656 | tf_op jit(solution)/shard_map/ppermute | solution.py:475
  28.1 4.0 %all-to-all-done.in_ref = bf16[8,128,384]{2,1,0:T(8,128)(2,1)S(1)} async-done(((bf16[8,128,384]{2,1,0:T(8,128)(2,1)}), bf16[8,128,384]{2,1,0:T(8,128)(2,1)S(1)}, u32[]{:S(2)}, u32[]{:S(2)}) %all-to-all-start) | async-done | bytes 786464 | tf_op jit(solution)/shard_map/all_to_all | solution.py:499
  32.1 1.4 %scan_state.1 = (f32[8,8,128]{2,1,0:T(8,128)S(1)}, f32[8,8,128]{2,1,0:T(8,128)S(1)}, f32[144,256]{1,0:T(8,128)S(1)}, bf16[2,80,256]{2,1,0:T(8,128)(2,1)S(1)}) custom-call(s32[4]{0:T(128)S(1)} %copy-done.5, s32[32]{0:T(128)S(1)} %copy-done.8, bf16[8,128,384]{2,1,0:T(8,128)(2,1)S(1)} %all-to-all-done.in_ref), custom_call_target="tpu_custom_call" | custom-call | flops 2200000 | bytes 6000 | tf_op jit(solution)/shard_map/scan_state/pallas_call | solution.py:524
  33.5 0.9 collective-permute-start.1
  34.4 0.9 collective-permute-done.1.got_ref.core_ref
  35.3 0.6 chip_state.1
  35.9 1.7 %collective-permute-start.2 = (bf16[80,256]{1,0:T(8,128)(2,1)S(1)}, bf16[80,256]{1,0:T(8,128)(2,1)S(1)}, u32[]{:S(2)}, u32[]{:S(2)}) collective-permute-start(bf16[80,256]{1,0:T(8,128)(2,1)S(1)} %get-tuple-element.82), channel_id=1, source_target_pairs={{0,16},{8,24},{16,0},{24,8},{32,48},{40,56},{48,32},{56,40},{64,80... | collective-permute-start | bytes 122888 | tf_op jit(solution)/shard_map/ppermute | solution.py:479
  37.6 4.7 %collective-permute-start.12 = (bf16[2,2,128,384]{3,2,1,0:T(8,128)(2,1)}, bf16[2,2,128,384]{3,2,1,0:T(8,128)(2,1)S(1)}, u32[]{:S(2)}, u32[]{:S(2)}) collective-permute-start(bf16[2,2,128,384]{3,2,1,0:T(8,128)(2,1)} %collective-permute-done.6.a_up), channel_id=1, source_target_pairs={{0,112},{8,120},{16,0},{24,8},{32,16},{40,24},{48,32},{56,40},{64,... | collective-permute-start | bytes 1179656 | tf_op jit(solution)/shard_map/ppermute | solution.py:475
  42.3 2.2 %scan_inside.2.y_ref = f32[2,1024,128]{2,1,0:T(8,128)S(1)} custom-call(s32[4]{0:T(128)S(1)} %copy-done.5, s32[32]{0:T(128)S(1)} %copy-done.8, bf16[8,128,384]{2,1,0:T(8,128)(2,1)S(1)} %all-to-all-done.in_ref), custom_call_target="tpu_custom_call" | custom-call | flops 2200000 | bytes 6000 | tf_op jit(solution)/shard_map/scan_inside/pallas_call | solution.py:543
  44.5 0.6 grow.3
  45.2 1.6 %attend_own.1 = (f32[2,8,256]{2,1,0:T(8,128)S(1)}, f32[2,8,256]{2,1,0:T(8,128)S(1)}, f32[2,3,128,256]{3,2,1,0:T(8,128)S(1)}, bf16[2,2,128,384]{3,2,1,0:T(8,128)(2,1)S(1)}) custom-call(s32[4]{0:T(128)S(1)} %copy-done.5, s32[32,32]{1,0:T(8,128)S(1)} %copy-done.4, bf16[3,128,384]{2,1,0:T(8,128)(2,1)S(1)} %copy-done.1, ...), custom_call_target="tpu_custom_call" | custom-call | flops 2200000 | bytes 6000 | tf_op jit(solution)/shard_map/attend_own/pallas_call | solution.py:554
  46.9 2.7 %collective-permute-start.14 = (bf16[2,2,128,384]{3,2,1,0:T(8,128)(2,1)}, bf16[2,2,128,384]{3,2,1,0:T(8,128)(2,1)}, u32[]{:S(2)}, u32[]{:S(2)}) collective-permute-start(bf16[2,2,128,384]{3,2,1,0:T(8,128)(2,1)} %collective-permute-done.8.b_up), channel_id=1, source_target_pairs={{0,112},{8,120},{16,0},{24,8},{32,16},{40,24},{48,32},{56,40},{64,... | collective-permute-start | bytes 1179656 | tf_op jit(solution)/shard_map/ppermute | solution.py:475
  49.7 2.8 %attend_step.3 = (f32[2,8,256]{2,1,0:T(8,128)S(1)}, f32[2,8,256]{2,1,0:T(8,128)S(1)}, f32[2,3,128,256]{3,2,1,0:T(8,128)S(1)}) custom-call(s32[4]{0:T(128)S(1)} %copy-done.5, s32[32,32]{1,0:T(8,128)S(1)} %copy-done.4, bf16[2,2,128,384]{3,2,1,0:T(8,128)(2,1)S(1)} %get-tuple-element.94.q_ref, bf16[2,2,128,384]{3,2,1,0:T(8,128)(2,1)} %collective-permute-done.6.a_up, ...), custom_call_target="tpu_custom_call" | custom-call | flops 2750000 | bytes 7500 | tf_op jit(solution)/shard_map/attend_step/pallas_call | solution.py:514
  52.5 4.4 %scan_inside.3.z_ref = f32[2,1024,128]{2,1,0:T(8,128)S(1)} custom-call(s32[4]{0:T(128)S(1)} %copy-done.5, s32[32]{0:T(128)S(1)} %copy-done.8, bf16[8,128,384]{2,1,0:T(8,128)(2,1)S(1)} %all-to-all-done.in_ref), custom_call_target="tpu_custom_call" | custom-call | flops 4400000 | bytes 12000 | tf_op jit(solution)/shard_map/scan_inside/pallas_call | solution.py:560
  56.8 2.9 %collective-permute-done.3.got_ref = bf16[80,256]{1,0:T(8,128)(2,1)S(1)} collective-permute-done((bf16[80,256]{1,0:T(8,128)(2,1)S(1)}, bf16[80,256]{1,0:T(8,128)(2,1)S(1)}, u32[]{:S(2)}, u32[]{:S(2)}) %collective-permute-start.3) | collective-permute-done | bytes 40992 | tf_op jit(solution)/shard_map/ppermute | solution.py:479
  59.7 0.6 grow.4
  60.3 3.6 %collective-permute-start.10 = (bf16[80,256]{1,0:T(8,128)(2,1)S(1)}, bf16[80,256]{1,0:T(8,128)(2,1)S(1)}, u32[]{:S(2)}, u32[]{:S(2)}) collective-permute-start(bf16[80,256]{1,0:T(8,128)(2,1)S(1)} %get-tuple-element.110), channel_id=1, source_target_pairs={{0,112},{8,120},{16,96},{24,104},{32,80},{40,88},{48,64},{56,72},{... | collective-permute-start | bytes 122888 | tf_op jit(solution)/shard_map/ppermute | solution.py:479
  64.0 1.7 %collective-permute-done.10.got_ref = bf16[80,256]{1,0:T(8,128)(2,1)S(1)} collective-permute-done((bf16[80,256]{1,0:T(8,128)(2,1)S(1)}, bf16[80,256]{1,0:T(8,128)(2,1)S(1)}, u32[]{:S(2)}, u32[]{:S(2)}) %collective-permute-start.10) | collective-permute-done | bytes 40992 | tf_op jit(solution)/shard_map/ppermute | solution.py:479
  65.6 1.2 %grow.5 = (f32[72,256]{1,0:T(8,128)S(1)}, f32[72,256]{1,0:T(8,128)}, bf16[80,256]{1,0:T(8,128)(2,1)S(1)}) custom-call(s32[4]{0:T(128)S(1)} %copy-done.5, bf16[80,256]{1,0:T(8,128)(2,1)S(1)} %collective-permute-done.10.got_ref, f32[72,256]{1,0:T(8,128)S(1)} %get-tuple-element.111.total_in, f32[72,256]{1,0:T(8,128)S(1)} %get-tuple-element.112.rest_0_), custom_call_target="tpu_custom_call" | custom-call | flops 550000 | bytes 1500 | tf_op jit(solution)/shard_map/grow/pallas_call | solution.py:574
  66.9 0.8 collective-permute-start.20
  67.6 1.7 %collective-permute-start.11 = (bf16[80,256]{1,0:T(8,128)(2,1)S(1)}, bf16[80,256]{1,0:T(8,128)(2,1)S(1)}, u32[]{:S(2)}, u32[]{:S(2)}) collective-permute-start(bf16[80,256]{1,0:T(8,128)(2,1)S(1)} %get-tuple-element.113), channel_id=1, source_target_pairs={{0,128},{8,136},{16,144},{24,152},{32,160},{40,168},{48,176},{56,1... | collective-permute-start | bytes 122888 | tf_op jit(solution)/shard_map/ppermute | solution.py:479
  69.4 3.1 %collective-permute-start.18 = (bf16[2,2,128,384]{3,2,1,0:T(8,128)(2,1)}, bf16[2,2,128,384]{3,2,1,0:T(8,128)(2,1)}, u32[]{:S(2)}, u32[]{:S(2)}) collective-permute-start(bf16[2,2,128,384]{3,2,1,0:T(8,128)(2,1)} %collective-permute-done.13.a_down), channel_id=1, source_target_pairs={{0,16},{8,24},{16,32},{24,40},{32,48},{40,56},{48,64},{56,72},{64,... | collective-permute-start | bytes 1179656 | tf_op jit(solution)/shard_map/ppermute | solution.py:475
  72.4 2.7 %attend_step.4 = (f32[2,8,256]{2,1,0:T(8,128)S(1)}, f32[2,8,256]{2,1,0:T(8,128)S(1)}, f32[2,3,128,256]{3,2,1,0:T(8,128)S(1)}) custom-call(s32[4]{0:T(128)S(1)} %copy-done.5, s32[32,32]{1,0:T(8,128)S(1)} %copy-done.4, bf16[2,2,128,384]{3,2,1,0:T(8,128)(2,1)S(1)} %get-tuple-element.94.q_ref, bf16[2,2,128,384]{3,2,1,0:T(8,128)(2,1)S(1)} %collective-permute-done.12.a_up, ...), custom_call_target="tpu_custom_call" | custom-call | flops 2750000 | bytes 7500 | tf_op jit(solution)/shard_map/attend_step/pallas_call | solution.py:514
  75.1 0.9 copy-done.2
  77.1 1.4 %collective-permute-start.22 = (bf16[2,2,128,384]{3,2,1,0:T(8,128)(2,1)}, bf16[2,2,128,384]{3,2,1,0:T(8,128)(2,1)}, u32[]{:S(2)}, u32[]{:S(2)}) collective-permute-start(bf16[2,2,128,384]{3,2,1,0:T(8,128)(2,1)} %collective-permute-done.20.b_down), channel_id=1, source_target_pairs={{0,16},{8,24},{16,32},{24,40},{32,48},{40,56},{48,64},{56,72},{64,... | collective-permute-start | bytes 1179656 | tf_op jit(solution)/shard_map/ppermute | solution.py:475
  78.5 7.3 %collective-permute-start.16 = (bf16[64,256]{1,0:T(8,128)(2,1)S(1)}, bf16[64,256]{1,0:T(8,128)(2,1)S(1)}, u32[]{:S(2)}, u32[]{:S(2)}) collective-permute-start(bf16[64,256]{1,0:T(8,128)(2,1)S(1)} %last_before.1.before_ref), channel_id=1, source_target_pairs={{0,8},{8,0},{16,24},{24,16},{32,40},{40,32},{48,56},{56,48},{64,72... | collective-permute-start | bytes 98312 | tf_op jit(solution)/shard_map/ppermute | solution.py:479
  85.7 0.8 dynamic_slice.3
  86.6 2.4 %scan_finish.1 = bf16[8,192,128]{2,1,0:T(8,128)(2,1)S(1)} custom-call(s32[4]{0:T(128)S(1)} %copy-done.5, bf16[8,128,384]{2,1,0:T(8,128)(2,1)S(1)} %all-to-all-done.in_ref, f32[2,1024,128]{2,1,0:T(8,128)S(1)} %scan_inside.2.y_ref, f32[2,1024,128]{2,1,0:T(8,128)S(1)} %scan_inside.3.z_ref, f32[8,8,128]{2,1,0:T(8,128)S(1)} %get-tuple-element.105.row_ref, ...), custom_call_target="tpu_custom_call" | custom-call | flops 3300000 | bytes 9000 | tf_op jit(solution)/shard_map/scan_finish/pallas_call | solution.py:591
  89.0 0.7 copy-done
  89.8 3.6 %all-to-all-start.1 = ((bf16[8,192,128]{2,1,0:T(8,128)(2,1)}), bf16[8,192,128]{2,1,0:T(8,128)(2,1)S(1)}, u32[]{:S(2)}, u32[]{:S(2)}) async-start(bf16[8,192,128]{2,1,0:T(8,128)(2,1)} %copy-done), calls=%async_computation.1 | async-start | bytes 786432 | tf_op jit(solution)/shard_map/all_to_all | solution.py:603
  93.4 2.8 %attend_step.5 = (f32[2,8,256]{2,1,0:T(8,128)S(1)}, f32[2,8,256]{2,1,0:T(8,128)S(1)}, f32[2,3,128,256]{3,2,1,0:T(8,128)S(1)}) custom-call(s32[4]{0:T(128)S(1)} %copy-done.5, s32[32,32]{1,0:T(8,128)S(1)} %copy-done.4, bf16[2,2,128,384]{3,2,1,0:T(8,128)(2,1)S(1)} %get-tuple-element.94.q_ref, bf16[2,2,128,384]{3,2,1,0:T(8,128)(2,1)} %collective-permute-done.17.a_up, ...), custom_call_target="tpu_custom_call" | custom-call | flops 2750000 | bytes 7500 | tf_op jit(solution)/shard_map/attend_step/pallas_call | solution.py:514
  96.2 2.1 %attend_last.2 = (bf16[128,384]{1,0:T(8,128)(2,1)S(1)}, bf16[128,384]{1,0:T(8,128)(2,1)S(1)}) custom-call(s32[4]{0:T(128)S(1)} %copy-done.5, s32[32,32]{1,0:T(8,128)S(1)} %copy-done.4, bf16[2,2,128,384]{3,2,1,0:T(8,128)(2,1)S(1)} %get-tuple-element.94.q_ref, bf16[2,2,128,384]{3,2,1,0:T(8,128)(2,1)} %collective-permute-done.21.a_ref, ...), custom_call_target="tpu_custom_call" | custom-call | flops 2200000 | bytes 6000 | tf_op jit(solution)/shard_map/attend_last/pallas_call | solution.py:609
  98.3 2.1 %attend_last.3 = (bf16[128,384]{1,0:T(8,128)(2,1)S(1)}, bf16[128,384]{1,0:T(8,128)(2,1)S(1)}) custom-call(s32[4]{0:T(128)S(1)} %copy-done.5, s32[32,32]{1,0:T(8,128)S(1)} %copy-done.4, bf16[2,2,128,384]{3,2,1,0:T(8,128)(2,1)S(1)} %get-tuple-element.94.q_ref, bf16[2,2,128,384]{3,2,1,0:T(8,128)(2,1)} %collective-permute-done.21.a_ref, ...), custom_call_target="tpu_custom_call" | custom-call | flops 2200000 | bytes 6000 | tf_op jit(solution)/shard_map/attend_last/pallas_call | solution.py:609
  100.9 1.7 %collective-permute-start.24 = (bf16[128,384]{1,0:T(8,128)(2,1)S(1)}, bf16[128,384]{1,0:T(8,128)(2,1)S(1)}, u32[]{:S(2)}, u32[]{:S(2)}) collective-permute-start(bf16[128,384]{1,0:T(8,128)(2,1)S(1)} %get-tuple-element.149), channel_id=1, source_target_pairs={{0,128},{8,136},{16,144},{24,152},{32,160},{40,168},{48,176},{56,1... | collective-permute-start | bytes 294920 | tf_op jit(solution)/shard_map/ppermute | solution.py:479
  102.6 1.6 %collective-permute-start.25 = (bf16[128,384]{1,0:T(8,128)(2,1)S(1)}, bf16[128,384]{1,0:T(8,128)(2,1)S(1)}, u32[]{:S(2)}, u32[]{:S(2)}) collective-permute-start(bf16[128,384]{1,0:T(8,128)(2,1)S(1)} %get-tuple-element.150), channel_id=1, source_target_pairs={{0,136},{8,128},{16,152},{24,144},{32,168},{40,160},{48,184},{56,1... | collective-permute-start | bytes 294920 | tf_op jit(solution)/shard_map/ppermute | solution.py:479
  104.2 2.5 %collective-permute-done.24.rest_2_ = bf16[128,384]{1,0:T(8,128)(2,1)S(1)} collective-permute-done((bf16[128,384]{1,0:T(8,128)(2,1)S(1)}, bf16[128,384]{1,0:T(8,128)(2,1)S(1)}, u32[]{:S(2)}, u32[]{:S(2)}) %collective-permute-start.24) | collective-permute-done | bytes 98336 | tf_op jit(solution)/shard_map/ppermute | solution.py:479
  106.7 2.5 %collective-permute-done.25.rest_3_ = bf16[128,384]{1,0:T(8,128)(2,1)S(1)} collective-permute-done((bf16[128,384]{1,0:T(8,128)(2,1)S(1)}, bf16[128,384]{1,0:T(8,128)(2,1)S(1)}, u32[]{:S(2)}, u32[]{:S(2)}) %collective-permute-start.25) | collective-permute-done | bytes 98336 | tf_op jit(solution)/shard_map/ppermute | solution.py:479
  109.1 1.5 %add_up.1 = bf16[128,1536]{1,0:T(8,128)(2,1)} custom-call(s32[4]{0:T(128)S(1)} %copy-done.5, bf16[8,192,128]{2,1,0:T(8,128)(2,1)S(1)} %all-to-all-done.1.scan_ref, bf16[128,384]{1,0:T(8,128)(2,1)S(1)} %get-tuple-element.147.rest_0_, bf16[128,384]{1,0:T(8,128)(2,1)S(1)} %collective-permute-done.23.rest_1_, ...), custom_call_target="tpu_custom_call" | custom-call | flops 1650000 | bytes 4500 | tf_op jit(solution)/shard_map/add_up/pallas_call | solution.py:619
  (51 shorter events, 2.0 us)
Async XLA Ops:
  3.0 6.4 %collective-permute-start = (bf16[3,128,384]{2,1,0:T(8,128)(2,1)}, bf16[3,128,384]{2,1,0:T(8,128)(2,1)S(1)}, u32[]{:S(2)}, u32[]{:S(2)}) collective-permute-start(bf16[3,128,384]{2,1,0:T(8,128)(2,1)} %get-tuple-element.78), channel_id=1, source_target_pairs={{0,8},{8,0},{16,24},{24,16},{32,40},{40,32},{48,56},{56,48},{64,72... | collective-permute-start | bytes 884744 | tf_op jit(solution)/shard_map/ppermute | solution.py:479
  6.2 17.4 %collective-permute-start.4 = (bf16[3,128,384]{2,1,0:T(8,128)(2,1)}, bf16[3,128,384]{2,1,0:T(8,128)(2,1)S(1)}, u32[]{:S(2)}, u32[]{:S(2)}) collective-permute-start(bf16[3,128,384]{2,1,0:T(8,128)(2,1)} %get-tuple-element.92), channel_id=1, source_target_pairs={{0,128},{8,136},{16,144},{24,152},{32,160},{40,168},{48,176},{56,1... | collective-permute-start | bytes 884744 | tf_op jit(solution)/shard_map/ppermute | solution.py:479
  7.2 16.4 %collective-permute-start.5 = (bf16[3,128,384]{2,1,0:T(8,128)(2,1)}, bf16[3,128,384]{2,1,0:T(8,128)(2,1)S(1)}, u32[]{:S(2)}, u32[]{:S(2)}) collective-permute-start(bf16[3,128,384]{2,1,0:T(8,128)(2,1)} %get-tuple-element.93), channel_id=1, source_target_pairs={{0,136},{8,128},{16,152},{24,144},{32,168},{40,160},{48,184},{56,1... | collective-permute-start | bytes 884744 | tf_op jit(solution)/shard_map/ppermute | solution.py:479
  11.3 3.7 %copy-start.1 = (bf16[3,128,384]{2,1,0:T(8,128)(2,1)S(1)}, bf16[3,128,384]{2,1,0:T(8,128)(2,1)}, u32[]{:S(2)}) copy-start(bf16[3,128,384]{2,1,0:T(8,128)(2,1)} %get-tuple-element.90.own) | copy-start | bytes 884740
  11.3 20.8 %all-to-all-start = ((bf16[8,128,384]{2,1,0:T(8,128)(2,1)}), bf16[8,128,384]{2,1,0:T(8,128)(2,1)S(1)}, u32[]{:S(2)}, u32[]{:S(2)}) async-start(bf16[8,128,384]{2,1,0:T(8,128)(2,1)} %scan_pack.1), calls=%async_computation | async-start | bytes 1572864 | tf_op jit(solution)/shard_map/all_to_all | solution.py:499
  15.1 22.5 %collective-permute-start.6 = (bf16[2,2,128,384]{3,2,1,0:T(8,128)(2,1)S(1)}, bf16[2,2,128,384]{3,2,1,0:T(8,128)(2,1)}, u32[]{:S(2)}, u32[]{:S(2)}) collective-permute-start(bf16[2,2,128,384]{3,2,1,0:T(8,128)(2,1)S(1)} %pad_maximum_fusion), channel_id=1, source_target_pairs={{0,112},{8,120},{16,0},{24,8},{32,16},{40,24},{48,32},{56,40},{64,... | collective-permute-start | bytes 1179656 | tf_op jit(solution)/shard_map/ppermute | solution.py:475
  20.6 21.7 %collective-permute-start.7 = (bf16[2,2,128,384]{3,2,1,0:T(8,128)(2,1)S(1)}, bf16[2,2,128,384]{3,2,1,0:T(8,128)(2,1)}, u32[]{:S(2)}, u32[]{:S(2)}) collective-permute-start(bf16[2,2,128,384]{3,2,1,0:T(8,128)(2,1)S(1)} %pad_maximum_fusion), channel_id=1, source_target_pairs={{0,16},{8,24},{16,32},{24,40},{32,48},{40,56},{48,64},{56,72},{64,... | collective-permute-start | bytes 1179656 | tf_op jit(solution)/shard_map/ppermute | solution.py:475
  23.6 8.5 %copy-start.5 = (s32[4]{0:T(128)S(1)}, s32[4]{0:T(128)}, u32[]{:S(2)}) copy-start(s32[4]{0:T(128)} %pad_add_fusion.ids) | copy-start | bytes 52
  23.6 8.5 %copy-start.8 = (s32[32]{0:T(128)S(1)}, s32[32]{0:T(128)}, u32[]{:S(2)}) copy-start(s32[32]{0:T(128)} %order_ref.5) | copy-start | bytes 388
  24.4 22.4 %collective-permute-start.8 = (bf16[2,2,128,384]{3,2,1,0:T(8,128)(2,1)}, bf16[2,2,128,384]{3,2,1,0:T(8,128)(2,1)}, u32[]{:S(2)}, u32[]{:S(2)}) collective-permute-start(bf16[2,2,128,384]{3,2,1,0:T(8,128)(2,1)} %pad_maximum_fusion.1), channel_id=1, source_target_pairs={{0,112},{8,120},{16,0},{24,8},{32,16},{40,24},{48,32},{56,40},{64,... | collective-permute-start | bytes 1179656 | tf_op jit(solution)/shard_map/ppermute | solution.py:475
  28.1 18.8 %collective-permute-start.9 = (bf16[2,2,128,384]{3,2,1,0:T(8,128)(2,1)}, bf16[2,2,128,384]{3,2,1,0:T(8,128)(2,1)}, u32[]{:S(2)}, u32[]{:S(2)}) collective-permute-start(bf16[2,2,128,384]{3,2,1,0:T(8,128)(2,1)} %pad_maximum_fusion.1), channel_id=1, source_target_pairs={{0,16},{8,24},{16,32},{24,40},{32,48},{40,56},{48,64},{56,72},{64,... | collective-permute-start | bytes 1179656 | tf_op jit(solution)/shard_map/ppermute | solution.py:475
  33.5 2.4 %copy-start.6 = (f32[8,8,128]{2,1,0:T(8,128)}, f32[8,8,128]{2,1,0:T(8,128)S(1)}, u32[]{:S(2)}) copy-start(f32[8,8,128]{2,1,0:T(8,128)S(1)} %get-tuple-element.106.col_ref) | copy-start | bytes 98308
  33.5 1.8 %collective-permute-start.1 = (bf16[2,80,256]{2,1,0:T(8,128)(2,1)S(1)}, bf16[2,80,256]{2,1,0:T(8,128)(2,1)S(1)}, u32[]{:S(2)}, u32[]{:S(2)}) collective-permute-start(bf16[2,80,256]{2,1,0:T(8,128)(2,1)S(1)} %get-tuple-element.81), channel_id=1, source_target_pairs={{0,8},{8,0},{16,24},{24,16},{32,40},{40,32},{48,56},{56,48},{64,72... | collective-permute-start | bytes 245768 | tf_op jit(solution)/shard_map/ppermute | solution.py:479
  35.9 8.6 %collective-permute-start.2 = (bf16[80,256]{1,0:T(8,128)(2,1)S(1)}, bf16[80,256]{1,0:T(8,128)(2,1)S(1)}, u32[]{:S(2)}, u32[]{:S(2)}) collective-permute-start(bf16[80,256]{1,0:T(8,128)(2,1)S(1)} %get-tuple-element.82), channel_id=1, source_target_pairs={{0,16},{8,24},{16,0},{24,8},{32,48},{40,56},{48,32},{56,40},{64,80... | collective-permute-start | bytes 122888 | tf_op jit(solution)/shard_map/ppermute | solution.py:479
  37.6 26.3 %collective-permute-start.12 = (bf16[2,2,128,384]{3,2,1,0:T(8,128)(2,1)}, bf16[2,2,128,384]{3,2,1,0:T(8,128)(2,1)S(1)}, u32[]{:S(2)}, u32[]{:S(2)}) collective-permute-start(bf16[2,2,128,384]{3,2,1,0:T(8,128)(2,1)} %collective-permute-done.6.a_up), channel_id=1, source_target_pairs={{0,112},{8,120},{16,0},{24,8},{32,16},{40,24},{48,32},{56,40},{64,... | collective-permute-start | bytes 1179656 | tf_op jit(solution)/shard_map/ppermute | solution.py:475
  42.3 21.6 %collective-permute-start.13 = (bf16[2,2,128,384]{3,2,1,0:T(8,128)(2,1)}, bf16[2,2,128,384]{3,2,1,0:T(8,128)(2,1)}, u32[]{:S(2)}, u32[]{:S(2)}) collective-permute-start(bf16[2,2,128,384]{3,2,1,0:T(8,128)(2,1)} %collective-permute-done.7.a_down), channel_id=1, source_target_pairs={{0,16},{8,24},{16,32},{24,40},{32,48},{40,56},{48,64},{56,72},{64,... | collective-permute-start | bytes 1179656 | tf_op jit(solution)/shard_map/ppermute | solution.py:475
  44.5 0.7 copy-start.4
  46.9 19.9 %collective-permute-start.14 = (bf16[2,2,128,384]{3,2,1,0:T(8,128)(2,1)}, bf16[2,2,128,384]{3,2,1,0:T(8,128)(2,1)}, u32[]{:S(2)}, u32[]{:S(2)}) collective-permute-start(bf16[2,2,128,384]{3,2,1,0:T(8,128)(2,1)} %collective-permute-done.8.b_up), channel_id=1, source_target_pairs={{0,112},{8,120},{16,0},{24,8},{32,16},{40,24},{48,32},{56,40},{64,... | collective-permute-start | bytes 1179656 | tf_op jit(solution)/shard_map/ppermute | solution.py:475
  49.7 17.2 %collective-permute-start.15 = (bf16[2,2,128,384]{3,2,1,0:T(8,128)(2,1)}, bf16[2,2,128,384]{3,2,1,0:T(8,128)(2,1)S(1)}, u32[]{:S(2)}, u32[]{:S(2)}) collective-permute-start(bf16[2,2,128,384]{3,2,1,0:T(8,128)(2,1)} %collective-permute-done.9.b_down), channel_id=1, source_target_pairs={{0,16},{8,24},{16,32},{24,40},{32,48},{40,56},{48,64},{56,72},{64,... | collective-permute-start | bytes 1179656 | tf_op jit(solution)/shard_map/ppermute | solution.py:475
  49.7 10.1 %collective-permute-start.3 = (bf16[80,256]{1,0:T(8,128)(2,1)S(1)}, bf16[80,256]{1,0:T(8,128)(2,1)S(1)}, u32[]{:S(2)}, u32[]{:S(2)}) collective-permute-start(bf16[80,256]{1,0:T(8,128)(2,1)S(1)} %get-tuple-element.87), channel_id=1, source_target_pairs={{0,32},{8,40},{16,48},{24,56},{32,0},{40,8},{48,16},{56,24},{64,96... | collective-permute-start | bytes 122888 | tf_op jit(solution)/shard_map/ppermute | solution.py:479
  60.3 5.3 %collective-permute-start.10 = (bf16[80,256]{1,0:T(8,128)(2,1)S(1)}, bf16[80,256]{1,0:T(8,128)(2,1)S(1)}, u32[]{:S(2)}, u32[]{:S(2)}) collective-permute-start(bf16[80,256]{1,0:T(8,128)(2,1)S(1)} %get-tuple-element.110), channel_id=1, source_target_pairs={{0,112},{8,120},{16,96},{24,104},{32,80},{40,88},{48,64},{56,72},{... | collective-permute-start | bytes 122888 | tf_op jit(solution)/shard_map/ppermute | solution.py:479
  63.9 12.7 %collective-permute-start.17 = (bf16[2,2,128,384]{3,2,1,0:T(8,128)(2,1)S(1)}, bf16[2,2,128,384]{3,2,1,0:T(8,128)(2,1)}, u32[]{:S(2)}, u32[]{:S(2)}) collective-permute-start(bf16[2,2,128,384]{3,2,1,0:T(8,128)(2,1)S(1)} %collective-permute-done.12.a_up), channel_id=1, source_target_pairs={{0,112},{8,120},{16,0},{24,8},{32,16},{40,24},{48,32},{56,40},{64,... | collective-permute-start | bytes 1179656 | tf_op jit(solution)/shard_map/ppermute | solution.py:475
  66.9 9.8 %collective-permute-start.20 = (bf16[2,2,128,384]{3,2,1,0:T(8,128)(2,1)S(1)}, bf16[2,2,128,384]{3,2,1,0:T(8,128)(2,1)}, u32[]{:S(2)}, u32[]{:S(2)}) collective-permute-start(bf16[2,2,128,384]{3,2,1,0:T(8,128)(2,1)S(1)} %collective-permute-done.15.b_down), channel_id=1, source_target_pairs={{0,16},{8,24},{16,32},{24,40},{32,48},{40,56},{48,64},{56,72},{64,... | collective-permute-start | bytes 1179656 | tf_op jit(solution)/shard_map/ppermute | solution.py:475
  67.6 8.4 %collective-permute-start.11 = (bf16[80,256]{1,0:T(8,128)(2,1)S(1)}, bf16[80,256]{1,0:T(8,128)(2,1)S(1)}, u32[]{:S(2)}, u32[]{:S(2)}) collective-permute-start(bf16[80,256]{1,0:T(8,128)(2,1)S(1)} %get-tuple-element.113), channel_id=1, source_target_pairs={{0,128},{8,136},{16,144},{24,152},{32,160},{40,168},{48,176},{56,1... | collective-permute-start | bytes 122888 | tf_op jit(solution)/shard_map/ppermute | solution.py:479
  69.4 24.0 %collective-permute-start.18 = (bf16[2,2,128,384]{3,2,1,0:T(8,128)(2,1)}, bf16[2,2,128,384]{3,2,1,0:T(8,128)(2,1)}, u32[]{:S(2)}, u32[]{:S(2)}) collective-permute-start(bf16[2,2,128,384]{3,2,1,0:T(8,128)(2,1)} %collective-permute-done.13.a_down), channel_id=1, source_target_pairs={{0,16},{8,24},{16,32},{24,40},{32,48},{40,56},{48,64},{56,72},{64,... | collective-permute-start | bytes 1179656 | tf_op jit(solution)/shard_map/ppermute | solution.py:475
  72.4 20.9 %collective-permute-start.19 = (bf16[2,2,128,384]{3,2,1,0:T(8,128)(2,1)}, bf16[2,2,128,384]{3,2,1,0:T(8,128)(2,1)}, u32[]{:S(2)}, u32[]{:S(2)}) collective-permute-start(bf16[2,2,128,384]{3,2,1,0:T(8,128)(2,1)} %collective-permute-done.14.b_up), channel_id=1, source_target_pairs={{0,112},{8,120},{16,0},{24,8},{32,16},{40,24},{48,32},{56,40},{64,... | collective-permute-start | bytes 1179656 | tf_op jit(solution)/shard_map/ppermute | solution.py:475
  75.1 0.9 copy-start.2
  76.6 10.0 %copy-start.7 = (f32[8,8,128]{2,1,0:T(8,128)S(1)}, f32[8,8,128]{2,1,0:T(8,128)}, u32[]{:S(2)}) copy-start(f32[8,8,128]{2,1,0:T(8,128)} %copy-done.6) | copy-start | bytes 98308
  76.6 19.6 %collective-permute-start.21 = (bf16[2,2,128,384]{3,2,1,0:T(8,128)(2,1)}, bf16[2,2,128,384]{3,2,1,0:T(8,128)(2,1)}, u32[]{:S(2)}, u32[]{:S(2)}) collective-permute-start(bf16[2,2,128,384]{3,2,1,0:T(8,128)(2,1)} %collective-permute-done.17.a_up), channel_id=1, source_target_pairs={{0,112},{8,120},{16,0},{24,8},{32,16},{40,24},{48,32},{56,40},{64,... | collective-permute-start | bytes 1179656 | tf_op jit(solution)/shard_map/ppermute | solution.py:475
  77.1 19.1 %collective-permute-start.22 = (bf16[2,2,128,384]{3,2,1,0:T(8,128)(2,1)}, bf16[2,2,128,384]{3,2,1,0:T(8,128)(2,1)}, u32[]{:S(2)}, u32[]{:S(2)}) collective-permute-start(bf16[2,2,128,384]{3,2,1,0:T(8,128)(2,1)} %collective-permute-done.20.b_down), channel_id=1, source_target_pairs={{0,16},{8,24},{16,32},{24,40},{32,48},{40,56},{48,64},{56,72},{64,... | collective-permute-start | bytes 1179656 | tf_op jit(solution)/shard_map/ppermute | solution.py:475
  78.5 8.1 %collective-permute-start.16 = (bf16[64,256]{1,0:T(8,128)(2,1)S(1)}, bf16[64,256]{1,0:T(8,128)(2,1)S(1)}, u32[]{:S(2)}, u32[]{:S(2)}) collective-permute-start(bf16[64,256]{1,0:T(8,128)(2,1)S(1)} %last_before.1.before_ref), channel_id=1, source_target_pairs={{0,8},{8,0},{16,24},{24,16},{32,40},{40,32},{48,56},{56,48},{64,72... | collective-permute-start | bytes 98312 | tf_op jit(solution)/shard_map/ppermute | solution.py:479
  89.0 0.7 copy-start
  89.8 3.6 %copy-start.3 = (f32[2,3,128,256]{3,2,1,0:T(8,128)S(1)}, f32[2,3,128,256]{3,2,1,0:T(8,128)}, u32[]{:S(2)}) copy-start(f32[2,3,128,256]{3,2,1,0:T(8,128)} %copy-done.2) | copy-start | bytes 2359300
  89.8 14.5 %all-to-all-start.1 = ((bf16[8,192,128]{2,1,0:T(8,128)(2,1)}), bf16[8,192,128]{2,1,0:T(8,128)(2,1)S(1)}, u32[]{:S(2)}, u32[]{:S(2)}) async-start(bf16[8,192,128]{2,1,0:T(8,128)(2,1)} %copy-done), calls=%async_computation.1 | async-start | bytes 786432 | tf_op jit(solution)/shard_map/all_to_all | solution.py:603
  100.5 3.7 %collective-permute-start.23 = (bf16[128,384]{1,0:T(8,128)(2,1)S(1)}, bf16[128,384]{1,0:T(8,128)(2,1)S(1)}, u32[]{:S(2)}, u32[]{:S(2)}) collective-permute-start(bf16[128,384]{1,0:T(8,128)(2,1)S(1)} %get-tuple-element.148), channel_id=1, source_target_pairs={{0,8},{8,0},{16,24},{24,16},{32,40},{40,32},{48,56},{56,48},{64,72... | collective-permute-start | bytes 294920 | tf_op jit(solution)/shard_map/ppermute | solution.py:479
  100.9 5.8 %collective-permute-start.24 = (bf16[128,384]{1,0:T(8,128)(2,1)S(1)}, bf16[128,384]{1,0:T(8,128)(2,1)S(1)}, u32[]{:S(2)}, u32[]{:S(2)}) collective-permute-start(bf16[128,384]{1,0:T(8,128)(2,1)S(1)} %get-tuple-element.149), channel_id=1, source_target_pairs={{0,128},{8,136},{16,144},{24,152},{32,160},{40,168},{48,176},{56,1... | collective-permute-start | bytes 294920 | tf_op jit(solution)/shard_map/ppermute | solution.py:479
  102.6 6.5 %collective-permute-start.25 = (bf16[128,384]{1,0:T(8,128)(2,1)S(1)}, bf16[128,384]{1,0:T(8,128)(2,1)S(1)}, u32[]{:S(2)}, u32[]{:S(2)}) collective-permute-start(bf16[128,384]{1,0:T(8,128)(2,1)S(1)} %get-tuple-element.150), channel_id=1, source_target_pairs={{0,136},{8,128},{16,152},{24,144},{32,168},{40,160},{48,184},{56,1... | collective-permute-start | bytes 294920 | tf_op jit(solution)/shard_map/ppermute | solution.py:479
